TPU v7x, 256 devices: a whole 4x4x8 slice. The times are simulated.
256 devices in a mesh: dp: 8 (over x, z_hi), expert: 32 (over y, z_lo, core).
Axes of the slice: x: 4, y: 4, z: 8 (z_hi: 2, z_lo: 4; z = z_hi * 4 + z_lo), core: 2. Of those that a mesh axis runs over, the one named last changes fastest.
Arguments:
- tokens: bfloat16 [32768, 2048], P(('dp', 'expert')), may hold values from -6 to 6
- route_ids: int32 [32768, 2], P(('dp', 'expert')), may hold values from 0 to 31, all different within a row; in each aligned block of 128 rows (0 to 127, 128 to 255, ...) at most 16 rows name the same one
- route_gates: float32 [32768, 2], P(('dp', 'expert')), may hold values from 0.05 to 0.5
- cotangent: bfloat16 [32768, 2048], P(('dp', 'expert')), may hold values from -6 to 6
- old_owner: int32 [32], replicated, may hold values from 0 to 31, each once
- new_owner: int32 [32], replicated, may hold values from 0 to 31, each once
- weight_in: bfloat16 [32, 2048, 768], P('expert'), may hold values from -0.125 to 0.125
- weight_out: bfloat16 [32, 768, 2048], P('expert'), may hold values from -0.21875 to 0.21875
- mean_in: bfloat16 [32, 2048, 768], P('expert', 'dp'), may hold values from -3 to 3
- square_in: bfloat16 [32, 2048, 768], P('expert', 'dp'), may hold values from 0.099609375 to 2
- mean_out: bfloat16 [32, 768, 2048], P('expert', 'dp'), may hold values from -3 to 3
- square_out: bfloat16 [32, 768, 2048], P('expert', 'dp'), may hold values from 0.099609375 to 2
Outputs:
- mixed: bfloat16 [32768, 2048], P(('dp', 'expert'))
- new_weight_in: bfloat16 [32, 2048, 768], P('expert', 'dp')
- new_mean_in: bfloat16 [32, 2048, 768], P('expert', 'dp')
- new_square_in: bfloat16 [32, 2048, 768], P('expert', 'dp')
- new_weight_out: bfloat16 [32, 768, 2048], P('expert', 'dp')
- new_mean_out: bfloat16 [32, 768, 2048], P('expert', 'dp')
- new_square_out: bfloat16 [32, 768, 2048], P('expert', 'dp')
Inputs may be any that keep to these rules, and one draw needn't show every extreme that they name: `route_ids`: each token names 2 different experts. The tokens of one device (aligned blocks of 128 tokens) name any one expert at most 16 times, a bound that some block reaches. `old_owner`: A permutation of the expert axis's indices. `new_owner`: A permutation of the expert axis's indices.
All inputs are finite; a program needn't handle non-finite values.
Results may differ from a plain program's by a relative error of at most 0.025.
Values may be sent and summed in bfloat16 or wider, within the bound.
A program may use at most 128 MiB of HBM per device.

v0:
```python
import jax
import jax.numpy as jnp
from jax import lax
from jax.sharding import PartitionSpec as P

beta_one = 0.9
beta_two = 0.95
adam_eps = 1e-08
learn_rate = 0.01
adam_step = 100.0


def silu_slope(preact):
    logistic = jax.nn.sigmoid(preact)
    return logistic * (1.0 + preact * (1.0 - logistic))


def adam_apply(weight, mean_old, square_old, gradient):
    mean_new = beta_one * mean_old.astype(jnp.float32) + (1.0 - beta_one) * gradient
    square_new = beta_two * square_old.astype(jnp.float32) + (1.0 - beta_two) * gradient * gradient
    stride = (
        mean_new
        / (1.0 - beta_one**adam_step)
        / (jnp.sqrt(square_new / (1.0 - beta_two**adam_step)) + adam_eps)
    )
    fresh = (weight.astype(jnp.float32) - learn_rate * stride).astype(jnp.bfloat16)
    return (fresh, mean_new.astype(jnp.bfloat16), square_new.astype(jnp.bfloat16))


def outer_dot(left, right):
    return lax.dot_general(
        left, right, (((0,), (0,)), ((), ())), preferred_element_type=jnp.float32
    )


def right_dot(left, right):
    return lax.dot_general(
        left, right, (((1,), (1,)), ((), ())), preferred_element_type=jnp.float32
    )


def body(
    tokens,
    route_ids,
    route_gates,
    cotangent,
    old_owner,
    new_owner,
    weight_in,
    weight_out,
    mean_in,
    square_in,
    mean_out,
    square_out,
):
    n_expert = lax.axis_size("expert")
    n_groups = lax.axis_size("dp")
    group = lax.axis_index("dp")
    tok_rows, width = tokens.shape
    picks_each = route_ids.shape[1]
    hidden_width = weight_in.shape[2]
    capacity = 2 * tok_rows * picks_each // n_expert
    slots_all = n_expert * capacity
    rows_in = width // n_groups
    rows_out = hidden_width // n_groups
    experts_all = jnp.arange(n_expert, dtype=jnp.int32)
    picked = (route_ids[:, :, None] == experts_all[None, None, :]).astype(jnp.int32)
    counts = jnp.sum(picked, axis=1)
    before = jnp.cumsum(counts, axis=0) - counts
    position = jnp.sum(picked * before[:, None, :], axis=2)
    old_slot = (jnp.sum(picked * old_owner, axis=2) * capacity + position).reshape(-1)
    new_slot = (jnp.sum(picked * new_owner, axis=2) * capacity + position).reshape(-1)
    holder = (new_owner[:, None] == experts_all[None, :]).astype(jnp.int32)
    source_of = jnp.sum(holder * old_owner[:, None], axis=0)
    spread = (
        lax.all_to_all(
            weight_in.reshape(n_expert, -1), "expert", split_axis=0, concat_axis=0, tiled=True
        ),
        lax.all_to_all(
            weight_out.reshape(n_expert, -1), "expert", split_axis=0, concat_axis=0, tiled=True
        ),
        lax.all_to_all(
            mean_in.reshape(n_expert, -1), "expert", split_axis=0, concat_axis=0, tiled=True
        ),
        lax.all_to_all(
            square_in.reshape(n_expert, -1), "expert", split_axis=0, concat_axis=0, tiled=True
        ),
        lax.all_to_all(
            mean_out.reshape(n_expert, -1), "expert", split_axis=0, concat_axis=0, tiled=True
        ),
        lax.all_to_all(
            square_out.reshape(n_expert, -1), "expert", split_axis=0, concat_axis=0, tiled=True
        ),
    )
    ordered = [jnp.take(piece, source_of, axis=0) for piece in spread]
    landed = (
        lax.all_to_all(ordered[0], "expert", split_axis=0, concat_axis=0, tiled=True),
        lax.all_to_all(ordered[1], "expert", split_axis=0, concat_axis=0, tiled=True),
        lax.all_to_all(ordered[2], "expert", split_axis=0, concat_axis=0, tiled=True),
        lax.all_to_all(ordered[3], "expert", split_axis=0, concat_axis=0, tiled=True),
        lax.all_to_all(ordered[4], "expert", split_axis=0, concat_axis=0, tiled=True),
        lax.all_to_all(ordered[5], "expert", split_axis=0, concat_axis=0, tiled=True),
    )
    in_full = landed[0].reshape(width, hidden_width)
    out_full = landed[1].reshape(hidden_width, width)
    in_share = lax.dynamic_slice_in_dim(in_full, group * rows_in, rows_in, 0)
    out_share = lax.dynamic_slice_in_dim(out_full, group * rows_out, rows_out, 0)
    moved_mean_in = landed[2].reshape(rows_in, hidden_width)
    moved_square_in = landed[3].reshape(rows_in, hidden_width)
    moved_mean_out = landed[4].reshape(rows_out, width)
    moved_square_out = landed[5].reshape(rows_out, width)
    copies = jnp.broadcast_to(tokens[:, None, :], (tok_rows, picks_each, width)).reshape(-1, width)
    sent = jnp.zeros((slots_all, width), jnp.bfloat16).at[old_slot].set(copies)
    arrived_rows = lax.all_to_all(
        sent.reshape(n_expert, capacity, width), "expert", split_axis=0, concat_axis=0, tiled=True
    ).reshape(slots_all, width)
    forward_preact = jnp.dot(arrived_rows, weight_in[0], preferred_element_type=jnp.float32)
    forward_hidden = jax.nn.silu(forward_preact).astype(jnp.bfloat16)
    produced = jnp.dot(forward_hidden, weight_out[0], preferred_element_type=jnp.float32).astype(
        jnp.bfloat16
    )
    returned = lax.all_to_all(
        produced.reshape(n_expert, capacity, width),
        "expert",
        split_axis=0,
        concat_axis=0,
        tiled=True,
    )
    gathered = returned.reshape(slots_all, width)[old_slot].reshape(tok_rows, picks_each, width)
    mixed = jnp.sum(route_gates[:, :, None] * gathered.astype(jnp.float32), axis=1).astype(
        jnp.bfloat16
    )
    scaled = (
        (route_gates[:, :, None] * cotangent[:, None, :].astype(jnp.float32))
        .astype(jnp.bfloat16)
        .reshape(-1, width)
    )
    rows_back = jnp.zeros((slots_all, width), jnp.bfloat16).at[new_slot].set(copies)
    grads_back = jnp.zeros((slots_all, width), jnp.bfloat16).at[new_slot].set(scaled)
    token_new, upstream = (
        lax.all_to_all(
            rows_back.reshape(n_expert, capacity, width),
            "expert",
            split_axis=0,
            concat_axis=0,
            tiled=True,
        ),
        lax.all_to_all(
            grads_back.reshape(n_expert, capacity, width),
            "expert",
            split_axis=0,
            concat_axis=0,
            tiled=True,
        ),
    )
    token_new = token_new.reshape(slots_all, width)
    upstream = upstream.reshape(slots_all, width)
    preact = jnp.dot(token_new, in_full, preferred_element_type=jnp.float32)
    downward = right_dot(upstream, out_full)
    hidden = jax.nn.silu(preact).astype(jnp.bfloat16)
    slope = (downward * silu_slope(preact)).astype(jnp.bfloat16)
    columns = token_new
    grad_in = lax.psum_scatter(
        outer_dot(columns, slope).astype(jnp.bfloat16), "dp", scatter_dimension=0, tiled=True
    ).astype(jnp.float32)
    columns = hidden
    grad_out = lax.psum_scatter(
        outer_dot(columns, upstream).astype(jnp.bfloat16), "dp", scatter_dimension=0, tiled=True
    ).astype(jnp.float32)
    fresh_in, next_mean_in, next_square_in = adam_apply(
        in_share, moved_mean_in, moved_square_in, grad_in
    )
    fresh_out, next_mean_out, next_square_out = adam_apply(
        out_share, moved_mean_out, moved_square_out, grad_out
    )
    return (
        mixed,
        fresh_in[None],
        next_mean_in[None],
        next_square_in[None],
        fresh_out[None],
        next_mean_out[None],
        next_square_out[None],
    )


def solution(mesh):
    return jax.shard_map(
        body,
        mesh=mesh,
        in_specs=(
            P(("dp", "expert"), None),
            P(("dp", "expert"), None),
            P(("dp", "expert"), None),
            P(("dp", "expert"), None),
            P(),
            P(),
            P("expert", None, None),
            P("expert", None, None),
            P("expert", "dp", None),
            P("expert", "dp", None),
            P("expert", "dp", None),
            P("expert", "dp", None),
        ),
        out_specs=(
            P(("dp", "expert"), None),
            P("expert", "dp", None),
            P("expert", "dp", None),
            P("expert", "dp", None),
            P("expert", "dp", None),
            P("expert", "dp", None),
            P("expert", "dp", None),
        ),
        check_vma=False,
    )
```

profile of v0, /device:TPU:4, one launch (start us, length us, event | category | flops | bytes accessed | tf_op | source)
XLA Modules:
  0.0 942.9 jit_solution(9751348668632854636)
XLA Ops:
  26.4 9.7 %all-to-all-done.12 = bf16[32,2,3072]{2,1,0:T(2,128)(2,1)S(1)} async-done(((bf16[32,2,3072]{2,1,0:T(2,128)(2,1)}), bf16[32,2,3072]{2,1,0:T(2,128)(2,1)S(1)}, u32[]{:S(2)}, u32[]{:S(2)}) %all-to-all-start.12) | async-done | bytes 393248 | tf_op jit(solution)/shard_map/all_to_all | solution.py:88
  44.7 9.3 all-to-all-done.10
  58.3 12.4 %all_to_all.132 = bf16[32,1,49152]{2,1,0:T(2,128)(2,1)} reshape(bf16[1,768,2048]{2,1,0:T(8,128)(2,1)} %param.23) | data formatting | bytes 6291456 | tf_op jit(solution)/shard_map/all_to_all | solution.py:79
  70.7 19.0 %reduce.15 = bf16[32,49152]{1,0:T(8,128)(2,1)S(1)} reduce(bf16[32,1,49152]{2,1,0:T(2,128)(2,1)} %all_to_all.132, bf16[]{:T(256)} %broadcast.145), dimensions={1}, to_apply=%all_to_all.132.reduce_sub_computation | reduce | bytes 6291458 | tf_op jit(solution)/shard_map/all_to_all | solution.py:79
  102.0 10.7 %all_to_all.130 = bf16[32,1,49152]{2,1,0:T(2,128)(2,1)} reshape(bf16[1,2048,768]{2,1,0:T(8,128)(2,1)} %param.22) | data formatting | bytes 6291456 | tf_op jit(solution)/shard_map/all_to_all | solution.py:76
  112.7 20.6 %reduce.16 = bf16[32,49152]{1,0:T(8,128)(2,1)} reduce(bf16[32,1,49152]{2,1,0:T(2,128)(2,1)} %all_to_all.130, bf16[]{:T(256)} %broadcast.145), dimensions={1}, to_apply=%all_to_all.130.reduce_sub_computation | reduce | bytes 6291458 | tf_op jit(solution)/shard_map/all_to_all | solution.py:76
  138.7 36.3 %all-to-all-done.8 = bf16[32,2,24576]{2,1,0:T(2,128)(2,1)S(1)} async-done(((bf16[32,2,24576]{2,1,0:T(2,128)(2,1)}), bf16[32,2,24576]{2,1,0:T(2,128)(2,1)S(1)}, u32[]{:S(2)}, u32[]{:S(2)}) %all-to-all-start.8) | async-done | bytes 3145760 | tf_op jit(solution)/shard_map/all_to_all | solution.py:79
  189.5 63.2 %all-to-all-done.2 = bf16[32,2,24576]{2,1,0:T(2,128)(2,1)} async-done(((bf16[32,2,24576]{2,1,0:T(2,128)(2,1)}), bf16[32,2,24576]{2,1,0:T(2,128)(2,1)}, u32[]{:S(2)}, u32[]{:S(2)}) %all-to-all-start.2) | async-done | bytes 3145760 | tf_op jit(solution)/shard_map/all_to_all | solution.py:76
  266.3 12.4 %reshape.344 = bf16[32,1,49152]{2,1,0:T(2,128)(2,1)} reshape(bf16[32,2,24576]{2,1,0:T(2,128)(2,1)S(1)} %all-to-all-done.8) | data formatting | bytes 6291456
  284.9 19.1 %reshape.340 = bf16[32,1,49152]{2,1,0:T(2,128)(2,1)} reshape(bf16[32,2,24576]{2,1,0:T(2,128)(2,1)} %all-to-all-done.2) | data formatting | bytes 6291456
  348.6 36.5 %all-to-all-done.6 = bf16[32,16,2048]{2,1,0:T(8,128)(2,1)} async-done(((bf16[32,16,2048]{2,1,0:T(8,128)(2,1)}), bf16[32,16,2048]{2,1,0:T(8,128)(2,1)}, u32[]{:S(2)}, u32[]{:S(2)}) %all-to-all-start.6) | async-done | bytes 2097184 | tf_op jit(solution)/shard_map/all_to_all | solution.py:141
  398.6 64.2 %all-to-all-done.3 = bf16[32,2,24576]{2,1,0:T(2,128)(2,1)} async-done(((bf16[32,2,24576]{2,1,0:T(2,128)(2,1)}), bf16[32,2,24576]{2,1,0:T(2,128)(2,1)}, u32[]{:S(2)}, u32[]{:S(2)}) %all-to-all-start.3) | async-done | bytes 3145760 | tf_op jit(solution)/shard_map/all_to_all | solution.py:97
  479.2 60.6 %all-to-all-done.9 = bf16[32,2,24576]{2,1,0:T(2,128)(2,1)S(1)} async-done(((bf16[32,2,24576]{2,1,0:T(2,128)(2,1)}), bf16[32,2,24576]{2,1,0:T(2,128)(2,1)S(1)}, u32[]{:S(2)}, u32[]{:S(2)}) %all-to-all-start.9) | async-done | bytes 3145760 | tf_op jit(solution)/shard_map/all_to_all | solution.py:98
  568.0 18.9 %reshape.342 = bf16[32,1,49152]{2,1,0:T(2,128)(2,1)} reshape(bf16[32,2,24576]{2,1,0:T(2,128)(2,1)} %all-to-all-done.3) | data formatting | bytes 6291456
  586.9 20.0 %reduce = bf16[32,49152]{1,0:T(8,128)(2,1)} reduce(bf16[32,1,49152]{2,1,0:T(2,128)(2,1)} %reshape.342, bf16[]{:T(256)} %constant.95), dimensions={1}, to_apply=%all_to_all.102.reduce_sub_computation | reduce | bytes 6291458 | tf_op jit(solution)/shard_map/all_to_all | solution.py:97
  611.8 12.4 %reshape.346 = bf16[32,1,49152]{2,1,0:T(2,128)(2,1)} reshape(bf16[32,2,24576]{2,1,0:T(2,128)(2,1)S(1)} %all-to-all-done.9) | data formatting | bytes 6291456
  624.2 18.3 %reduce.2 = bf16[32,49152]{1,0:T(8,128)(2,1)S(1)} reduce(bf16[32,1,49152]{2,1,0:T(2,128)(2,1)} %reshape.346, bf16[]{:T(256)} %constant.95), dimensions={1}, to_apply=%all_to_all.114.reduce_sub_computation | reduce | bytes 6291458 | tf_op jit(solution)/shard_map/all_to_all | solution.py:98
  673.0 20.4 %all-to-all-done.11 = bf16[32,2,3072]{2,1,0:T(2,128)(2,1)S(1)} async-done(((bf16[32,2,3072]{2,1,0:T(2,128)(2,1)}), bf16[32,2,3072]{2,1,0:T(2,128)(2,1)S(1)}, u32[]{:S(2)}, u32[]{:S(2)}) %all-to-all-start.11) | async-done | bytes 393248 | tf_op jit(solution)/shard_map/all_to_all | solution.py:100
  699.2 25.8 %all-to-all-done.5 = bf16[32,2,3072]{2,1,0:T(2,128)(2,1)S(1)} async-done(((bf16[32,2,3072]{2,1,0:T(2,128)(2,1)}), bf16[32,2,3072]{2,1,0:T(2,128)(2,1)S(1)}, u32[]{:S(2)}, u32[]{:S(2)}) %all-to-all-start.5) | async-done | bytes 393248 | tf_op jit(solution)/shard_map/all_to_all | solution.py:99
  733.6 10.3 %all-to-all-done.15 = bf16[32,2,3072]{2,1,0:T(2,128)(2,1)S(1)} async-done(((bf16[32,2,3072]{2,1,0:T(2,128)(2,1)}), bf16[32,2,3072]{2,1,0:T(2,128)(2,1)S(1)}, u32[]{:S(2)}, u32[]{:S(2)}) %all-to-all-start.15) | async-done | bytes 393248 | tf_op jit(solution)/shard_map/all_to_all | solution.py:102
  763.1 48.7 %all-to-all-done = bf16[32,16,2048]{2,1,0:T(8,128)(2,1)} async-done(((bf16[32,16,2048]{2,1,0:T(8,128)(2,1)}), bf16[32,16,2048]{2,1,0:T(8,128)(2,1)}, u32[]{:S(2)}, u32[]{:S(2)}) %all-to-all-start) | async-done | bytes 2097184 | tf_op jit(solution)/shard_map/all_to_all | solution.py:114
  811.8 9.6 %all-to-all-start.13 = ((bf16[32,2,3072]{2,1,0:T(2,128)(2,1)}), bf16[32,2,3072]{2,1,0:T(2,128)(2,1)}, u32[]{:S(2)}, u32[]{:S(2)}) async-start(bf16[32,2,3072]{2,1,0:T(2,128)(2,1)} %reshape.353), calls=%async_computation.14 | async-start | bytes 786432 | tf_op jit(solution)/shard_map/all_to_all | solution.py:101
  829.3 17.9 %all-to-all-done.13 = bf16[32,2,3072]{2,1,0:T(2,128)(2,1)} async-done(((bf16[32,2,3072]{2,1,0:T(2,128)(2,1)}), bf16[32,2,3072]{2,1,0:T(2,128)(2,1)}, u32[]{:S(2)}, u32[]{:S(2)}) %all-to-all-start.13) | async-done | bytes 393248 | tf_op jit(solution)/shard_map/all_to_all | solution.py:101
  882.0 41.0 %all-to-all-done.1 = bf16[32,16,2048]{2,1,0:T(8,128)(2,1)S(1)} async-done(((bf16[32,16,2048]{2,1,0:T(8,128)(2,1)}), bf16[32,16,2048]{2,1,0:T(8,128)(2,1)S(1)}, u32[]{:S(2)}, u32[]{:S(2)}) %all-to-all-start.1) | async-done | bytes 2097184 | tf_op jit(solution)/shard_map/all_to_all | solution.py:122
  (175 shorter events, 310.9 us)
Async XLA Ops:
  13.3 22.8 %all-to-all-start.12 = ((bf16[32,2,3072]{2,1,0:T(2,128)(2,1)}), bf16[32,2,3072]{2,1,0:T(2,128)(2,1)S(1)}, u32[]{:S(2)}, u32[]{:S(2)}) async-start(bf16[32,2,3072]{2,1,0:T(2,128)(2,1)} %reshape.351), calls=%async_computation.13 | async-start | bytes 786432 | tf_op jit(solution)/shard_map/all_to_all | solution.py:88
  22.2 17.8 %copy-start.22 = (bf16[1,96,2048]{2,1,0:T(8,128)(2,1)S(1)}, bf16[1,96,2048]{2,1,0:T(8,128)(2,1)}, u32[]{:S(2)}) copy-start(bf16[1,96,2048]{2,1,0:T(8,128)(2,1)} %param.27) | copy-start | bytes 1179652
  36.1 17.8 %copy-start.6 = (bf16[32,2,3072]{2,1,0:T(2,128)(2,1)}, bf16[32,2,3072]{2,1,0:T(2,128)(2,1)S(1)}, u32[]{:S(2)}) copy-start(bf16[32,2,3072]{2,1,0:T(2,128)(2,1)S(1)} %all-to-all-done.12) | copy-start | bytes 1179652
  36.1 17.8 %all-to-all-start.10 = ((bf16[32,2,3072]{2,1,0:T(2,128)(2,1)}), bf16[32,2,3072]{2,1,0:T(2,128)(2,1)S(1)}, u32[]{:S(2)}, u32[]{:S(2)}) async-start(bf16[32,2,3072]{2,1,0:T(2,128)(2,1)} %reshape.331), calls=%async_computation.11 | async-start | bytes 786432 | tf_op jit(solution)/shard_map/all_to_all | solution.py:85
  53.9 39.5 %all-to-all-start.14 = ((bf16[32,2,3072]{2,1,0:T(2,128)(2,1)}), bf16[32,2,3072]{2,1,0:T(2,128)(2,1)S(1)}, u32[]{:S(2)}, u32[]{:S(2)}) async-start(bf16[32,2,3072]{2,1,0:T(2,128)(2,1)} %reshape.347), calls=%async_computation.16 | async-start | bytes 786432 | tf_op jit(solution)/shard_map/all_to_all | solution.py:91
  94.2 80.8 %all-to-all-start.8 = ((bf16[32,2,24576]{2,1,0:T(2,128)(2,1)}), bf16[32,2,24576]{2,1,0:T(2,128)(2,1)S(1)}, u32[]{:S(2)}, u32[]{:S(2)}) async-start(bf16[32,2,24576]{2,1,0:T(2,128)(2,1)} %reshape.343), calls=%async_computation.8 | async-start | bytes 6291456 | tf_op jit(solution)/shard_map/all_to_all | solution.py:79
  138.7 41.1 %copy-start.23 = (s32[128,2]{0,1:T(2,128)S(1)}, s32[128,2]{0,1:T(2,128)}, u32[]{:S(2)}) copy-start(s32[128,2]{0,1:T(2,128)} %param.17) | copy-start | bytes 3076
  175.0 77.8 %all-to-all-start.2 = ((bf16[32,2,24576]{2,1,0:T(2,128)(2,1)}), bf16[32,2,24576]{2,1,0:T(2,128)(2,1)}, u32[]{:S(2)}, u32[]{:S(2)}) async-start(bf16[32,2,24576]{2,1,0:T(2,128)(2,1)} %reshape.339), calls=%async_computation.2 | async-start | bytes 6291456 | tf_op jit(solution)/shard_map/all_to_all | solution.py:76
  252.7 72.7 %all-to-all-start.4 = ((bf16[32,2,3072]{2,1,0:T(2,128)(2,1)}), bf16[32,2,3072]{2,1,0:T(2,128)(2,1)S(1)}, u32[]{:S(2)}, u32[]{:S(2)}) async-start(bf16[32,2,3072]{2,1,0:T(2,128)(2,1)} %reshape.335), calls=%async_computation.4 | async-start | bytes 786432 | tf_op jit(solution)/shard_map/all_to_all | solution.py:82
  326.2 58.9 %all-to-all-start.6 = ((bf16[32,16,2048]{2,1,0:T(8,128)(2,1)}), bf16[32,16,2048]{2,1,0:T(8,128)(2,1)}, u32[]{:S(2)}, u32[]{:S(2)}) async-start(bf16[32,16,2048]{2,1,0:T(8,128)(2,1)} %bitcast.79), calls=%async_computation.6 | async-start | bytes 4194304 | tf_op jit(solution)/shard_map/all_to_all | solution.py:141
  385.0 77.8 %all-to-all-start.3 = ((bf16[32,2,24576]{2,1,0:T(2,128)(2,1)}), bf16[32,2,24576]{2,1,0:T(2,128)(2,1)}, u32[]{:S(2)}, u32[]{:S(2)}) async-start(bf16[32,2,24576]{2,1,0:T(2,128)(2,1)} %reshape.341), calls=%async_computation.3 | async-start | bytes 6291456 | tf_op jit(solution)/shard_map/all_to_all | solution.py:97
  398.6 68.3 %copy-start.24 = (f32[128,2]{0,1:T(2,128)S(1)}, f32[128,2]{0,1:T(2,128)}, u32[]{:S(2)}) copy-start(f32[128,2]{0,1:T(2,128)} %param.18) | copy-start | bytes 3076
  462.8 77.0 %all-to-all-start.9 = ((bf16[32,2,24576]{2,1,0:T(2,128)(2,1)}), bf16[32,2,24576]{2,1,0:T(2,128)(2,1)S(1)}, u32[]{:S(2)}, u32[]{:S(2)}) async-start(bf16[32,2,24576]{2,1,0:T(2,128)(2,1)} %reshape.345), calls=%async_computation.9 | async-start | bytes 6291456 | tf_op jit(solution)/shard_map/all_to_all | solution.py:98
  539.8 111.4 %all-to-all-start.7 = ((bf16[32,16,2048]{2,1,0:T(8,128)(2,1)}), bf16[32,16,2048]{2,1,0:T(8,128)(2,1)}, u32[]{:S(2)}, u32[]{:S(2)}) async-start(bf16[32,16,2048]{2,1,0:T(8,128)(2,1)} %bitcast.78), calls=%async_computation.7 | async-start | bytes 4194304 | tf_op jit(solution)/shard_map/all_to_all | solution.py:148
  544.7 385.0 %reduce-scatter.3.cloned.1.call-start = ((), (), s32[]{:S(2)}) async-start(), calls=%async_computation.18 | async-start | bytes 3538944 | tf_op jit(solution)/shard_map/reduce_scatter | solution.py:163
  663.5 30.0 %all-to-all-start.11 = ((bf16[32,2,3072]{2,1,0:T(2,128)(2,1)}), bf16[32,2,3072]{2,1,0:T(2,128)(2,1)S(1)}, u32[]{:S(2)}, u32[]{:S(2)}) async-start(bf16[32,2,3072]{2,1,0:T(2,128)(2,1)} %reshape.333), calls=%async_computation.12 | async-start | bytes 786432 | tf_op jit(solution)/shard_map/all_to_all | solution.py:100
  693.5 31.6 %all-to-all-start.5 = ((bf16[32,2,3072]{2,1,0:T(2,128)(2,1)}), bf16[32,2,3072]{2,1,0:T(2,128)(2,1)S(1)}, u32[]{:S(2)}, u32[]{:S(2)}) async-start(bf16[32,2,3072]{2,1,0:T(2,128)(2,1)} %reshape.337), calls=%async_computation.5 | async-start | bytes 786432 | tf_op jit(solution)/shard_map/all_to_all | solution.py:99
  725.0 18.9 %copy-start.10 = (bf16[32,2,3072]{2,1,0:T(2,128)(2,1)}, bf16[32,2,3072]{2,1,0:T(2,128)(2,1)S(1)}, u32[]{:S(2)}) copy-start(bf16[32,2,3072]{2,1,0:T(2,128)(2,1)S(1)} %all-to-all-done.5) | copy-start | bytes 1179652
  725.0 18.9 %all-to-all-start.15 = ((bf16[32,2,3072]{2,1,0:T(2,128)(2,1)}), bf16[32,2,3072]{2,1,0:T(2,128)(2,1)S(1)}, u32[]{:S(2)}, u32[]{:S(2)}) async-start(bf16[32,2,3072]{2,1,0:T(2,128)(2,1)} %reshape.349), calls=%async_computation.17 | async-start | bytes 786432 | tf_op jit(solution)/shard_map/all_to_all | solution.py:102
  744.7 67.1 %all-to-all-start = ((bf16[32,16,2048]{2,1,0:T(8,128)(2,1)}), bf16[32,16,2048]{2,1,0:T(8,128)(2,1)}, u32[]{:S(2)}, u32[]{:S(2)}) async-start(bf16[32,16,2048]{2,1,0:T(8,128)(2,1)} %bitcast.1), calls=%async_computation | async-start | bytes 4194304 | tf_op jit(solution)/shard_map/all_to_all | solution.py:114
  752.9 180.1 %reduce-scatter.5.cloned.1.call-start = ((), (), s32[]{:S(2)}) async-start(), calls=%async_computation.19 | async-start | bytes 3538944 | tf_op jit(solution)/shard_map/reduce_scatter | solution.py:167
  758.3 63.2 %copy-start.2 = (bf16[1,768,2048]{2,1,0:T(8,128)(2,1)S(1)}, bf16[1,768,2048]{2,1,0:T(8,128)(2,1)}, u32[]{:S(2)}) copy-start(bf16[1,768,2048]{2,1,0:T(8,128)(2,1)} %param.23) | copy-start | bytes 9437188
  811.8 35.4 %all-to-all-start.13 = ((bf16[32,2,3072]{2,1,0:T(2,128)(2,1)}), bf16[32,2,3072]{2,1,0:T(2,128)(2,1)}, u32[]{:S(2)}, u32[]{:S(2)}) async-start(bf16[32,2,3072]{2,1,0:T(2,128)(2,1)} %reshape.353), calls=%async_computation.14 | async-start | bytes 786432 | tf_op jit(solution)/shard_map/all_to_all | solution.py:101
  847.2 75.8 %all-to-all-start.1 = ((bf16[32,16,2048]{2,1,0:T(8,128)(2,1)}), bf16[32,16,2048]{2,1,0:T(8,128)(2,1)S(1)}, u32[]{:S(2)}, u32[]{:S(2)}) async-start(bf16[32,16,2048]{2,1,0:T(8,128)(2,1)} %bitcast.80), calls=%async_computation.1 | async-start | bytes 4194304 | tf_op jit(solution)/shard_map/all_to_all | solution.py:122
  (22 other events, 98.8 us)
Sparse Core Ops, SparseCore 0:
  659.4 124.7 reduce-scatter.2
  789.0 126.0 reduce-scatter.4
where the time goes:
time: 956 us; the launch traced here: 943 us
  waiting for transfers between devices  444 us (46%)
  local copies, waits for them, and re-layouts  218 us (23%)
  other arithmetic  142 us (15%)
  starting transfers between devices  98.3 us (10%)
  matrix products  26.6 us (3%)
  between operations  14.8 us (2%)
    unnamed x87, local copies, waits for them, and re-layouts  127 us
    all_to_all x1, waiting for transfers between devices, body(): lax.all_to_all(ordered[0], 'expert', split_axis=0, concat_axis=0, tiled=T...  64.2 us
    all_to_all x1, waiting for transfers between devices, body(): lax.all_to_all(weight_in.reshape(n_expert, -1), 'expert', split_axis=0, c...  63.2 us
    all_to_all x1, waiting for transfers between devices, body(): lax.all_to_all(ordered[1], 'expert', split_axis=0, concat_axis=0, tiled=T...  60.6 us
    all_to_all x1, waiting for transfers between devices, body(): lax.all_to_all(sent.reshape(n_expert, capacity, width), 'expert', split_a...  48.7 us
    all_to_all x1, waiting for transfers between devices, body(): lax.all_to_all(produced.reshape(n_expert, capacity, width), 'expert', spl...  41 us
    all_to_all x1, waiting for transfers between devices, body(): lax.all_to_all(rows_back.reshape(n_expert, capacity, width), 'expert', sp...  36.5 us
    all_to_all x1, waiting for transfers between devices, body(): lax.all_to_all(weight_out.reshape(n_expert, -1), 'expert', split_axis=0,...  36.3 us
  transfers between devices with their start and end apart: 18, of which 13 were waited for; matrix products, arithmetic and copies ran while one was open for 36% of the time, Pallas kernels for 0%

commit v1 on v0

v1 whole, which is shorter than its diff:
```python
import jax
import jax.numpy as jnp
from jax import lax
from jax.sharding import PartitionSpec as P

beta_one = 0.9
beta_two = 0.95
adam_eps = 1e-08
learn_rate = 0.01
adam_step = 100.0


def silu_slope(preact):
    logistic = jax.nn.sigmoid(preact)
    return logistic * (1.0 + preact * (1.0 - logistic))


def adam_apply(weight, mean_old, square_old, gradient):
    mean_new = beta_one * mean_old.astype(jnp.float32) + (1.0 - beta_one) * gradient
    square_new = beta_two * square_old.astype(jnp.float32) + (1.0 - beta_two) * gradient * gradient
    stride = (
        mean_new
        / (1.0 - beta_one**adam_step)
        / (jnp.sqrt(square_new / (1.0 - beta_two**adam_step)) + adam_eps)
    )
    fresh = (weight.astype(jnp.float32) - learn_rate * stride).astype(jnp.bfloat16)
    return (fresh, mean_new.astype(jnp.bfloat16), square_new.astype(jnp.bfloat16))


def outer_dot(left, right):
    return lax.dot_general(
        left, right, (((0,), (0,)), ((), ())), preferred_element_type=jnp.float32
    )


def right_dot(left, right):
    return lax.dot_general(
        left, right, (((1,), (1,)), ((), ())), preferred_element_type=jnp.float32
    )


def body(
    tokens,
    route_ids,
    route_gates,
    cotangent,
    old_owner,
    new_owner,
    weight_in,
    weight_out,
    mean_in,
    square_in,
    mean_out,
    square_out,
):
    n_expert = lax.axis_size("expert")
    n_groups = lax.axis_size("dp")
    group = lax.axis_index("dp")
    tok_rows, width = tokens.shape
    picks_each = route_ids.shape[1]
    hidden_width = weight_in.shape[2]
    capacity = 2 * tok_rows * picks_each // n_expert
    slots_all = n_expert * capacity
    rows_in = width // n_groups
    rows_out = hidden_width // n_groups
    experts_all = jnp.arange(n_expert, dtype=jnp.int32)
    picked = (route_ids[:, :, None] == experts_all[None, None, :]).astype(jnp.int32)
    counts = jnp.sum(picked, axis=1)
    before = jnp.cumsum(counts, axis=0) - counts
    position = jnp.sum(picked * before[:, None, :], axis=2)
    slot = jnp.sum(picked * old_owner, axis=2) * capacity + position
    holder = (new_owner[:, None] == experts_all[None, :]).astype(jnp.int32)
    source_of = jnp.sum(holder * old_owner[:, None], axis=0)
    slot_ids = jnp.arange(slots_all, dtype=jnp.int32)
    place = [
        (slot[:, k][None, :] == slot_ids[:, None]).astype(jnp.bfloat16) for k in range(picks_each)
    ]

    def swap(rows):
        return lax.all_to_all(rows, "expert", split_axis=0, concat_axis=0, tiled=True)

    def exchange(rows):
        return swap(rows.reshape(n_expert, capacity, width)).reshape(slots_all, width)

    sent = jnp.dot(sum(place), tokens, preferred_element_type=jnp.float32).astype(jnp.bfloat16)
    arrived = exchange(sent)
    scaled = [
        (route_gates[:, k, None] * cotangent.astype(jnp.float32)).astype(jnp.bfloat16)
        for k in range(picks_each)
    ]
    graded = jnp.dot(
        jnp.concatenate(place, axis=1),
        jnp.concatenate(scaled, axis=0),
        preferred_element_type=jnp.float32,
    ).astype(jnp.bfloat16)
    upstream = exchange(graded)
    preact = jnp.dot(arrived, weight_in[0], preferred_element_type=jnp.float32)
    hidden = jax.nn.silu(preact).astype(jnp.bfloat16)
    produced = jnp.dot(hidden, weight_out[0], preferred_element_type=jnp.float32).astype(
        jnp.bfloat16
    )
    returned = exchange(produced)
    mixed = sum(
        route_gates[:, k, None] * outer_dot(place[k], returned) for k in range(picks_each)
    ).astype(jnp.bfloat16)
    downward = right_dot(upstream, weight_out[0])
    slope = (downward * silu_slope(preact)).astype(jnp.bfloat16)
    grad_out = lax.psum_scatter(
        outer_dot(hidden, upstream).astype(jnp.bfloat16), "dp", scatter_dimension=0, tiled=True
    ).astype(jnp.float32)
    grad_in = lax.psum_scatter(
        outer_dot(arrived, slope).astype(jnp.bfloat16), "dp", scatter_dimension=0, tiled=True
    ).astype(jnp.float32)
    in_share = lax.dynamic_slice_in_dim(weight_in[0], group * rows_in, rows_in, 0)
    out_share = lax.dynamic_slice_in_dim(weight_out[0], group * rows_out, rows_out, 0)
    after_in = adam_apply(in_share, mean_in[0], square_in[0], grad_in)
    after_out = adam_apply(out_share, mean_out[0], square_out[0], grad_out)
    lanes = 128
    deep = rows_in // n_expert
    wide = hidden_width // lanes
    tall = rows_out // 2
    cols = width // lanes

    def pieces_in(share):
        cut = share.reshape(n_expert, deep, wide, lanes).transpose(0, 2, 1, 3)
        return cut.reshape(n_expert, wide * deep, lanes)

    def joined_in(cut):
        share = cut.reshape(n_expert, wide, deep, lanes).transpose(0, 2, 1, 3)
        return share.reshape(1, rows_in, hidden_width)

    def pieces_out(share):
        cut = share.reshape(2, tall, cols, lanes).transpose(0, 2, 1, 3)
        return cut.reshape(n_expert, tall, lanes)

    def joined_out(cut):
        share = cut.reshape(2, cols, tall, lanes).transpose(0, 2, 1, 3)
        return share.reshape(1, rows_out, width)

    packed = jnp.concatenate(
        [pieces_in(part) for part in after_in] + [pieces_out(part) for part in after_out], axis=1
    )
    spread = swap(packed)
    landed = swap(jnp.take(spread, source_of, axis=0))
    moved = jnp.split(landed, 6, axis=1)
    return (
        mixed,
        joined_in(moved[0]),
        joined_in(moved[1]),
        joined_in(moved[2]),
        joined_out(moved[3]),
        joined_out(moved[4]),
        joined_out(moved[5]),
    )


def solution(mesh):
    return jax.shard_map(
        body,
        mesh=mesh,
        in_specs=(
            P(("dp", "expert"), None),
            P(("dp", "expert"), None),
            P(("dp", "expert"), None),
            P(("dp", "expert"), None),
            P(),
            P(),
            P("expert", None, None),
            P("expert", None, None),
            P("expert", "dp", None),
            P("expert", "dp", None),
            P("expert", "dp", None),
            P("expert", "dp", None),
        ),
        out_specs=(
            P(("dp", "expert"), None),
            P("expert", "dp", None),
            P("expert", "dp", None),
            P("expert", "dp", None),
            P("expert", "dp", None),
            P("expert", "dp", None),
            P("expert", "dp", None),
        ),
        check_vma=False,
    )
```

time: 956 us -> 551 us (0.58); the launches traced: 943 us -> 549 us
  local copies, waits for them, and re-layouts: 218 us -> 14.4 us
  other arithmetic: 142 us -> 11.9 us
  starting transfers between devices: 98.3 us -> 28 us
    reduce_scatter x2, waiting for transfers between devices: 0.01 us -> 209 us  [the longest x1 109 us: body(): lax.psum_scatter(outer_dot(arrived, slope).astype(jnp.bfloat16), 'dp', sc...]
    all_to_all x16 -> x5, waiting for transfers between devices: 444 us -> 241 us  [swap(): lax.all_to_all(rows, 'expert', split_axis=0, concat_axis=0, tiled=True)]
    unnamed x87 -> x27, local copies, waits for them, and re-layouts: 127 us -> 3.39 us
    all_to_all x16 -> x0, other arithmetic: 112 us -> none  [the longest x3 28.5 us: body(): lax.all_to_all(ordered[1], 'expert', split_axis=0, concat_axis=0, tiled=T...]
    all_to_all x16 -> x5, starting transfers between devices: 98 us -> 27.7 us  [swap(): lax.all_to_all(rows, 'expert', split_axis=0, concat_axis=0, tiled=True)]
    all_to_all x7 -> x0, local copies, waits for them, and re-layouts: 29.3 us -> none  [the longest x1 12.4 us: body(): lax.all_to_all(weight_out.reshape(n_expert, -1), 'expert', split_axis=0,...]
    gather x7 -> x1, local copies, waits for them, and re-layouts: 21 us -> 3.93 us  [body(): landed = swap(jnp.take(spread, source_of, axis=0))]
    mul x7 -> x1, local copies, waits for them, and re-layouts: 16 us -> 0.01 us  [body(): route_gates[:, k, None] * outer_dot(place[k], returned)]
  transfers between devices with their start and end apart: 18 -> 7, of which waited for: 13 -> 7; matrix products, arithmetic and copies ran while one was open for 36% -> 6% of each run, Pallas kernels for 0% -> 0%
where the time goes in v1:
time: 551 us; the launch traced here: 549 us
  waiting for transfers between devices  450 us (82%)
  matrix products  30.2 us (5%)
  starting transfers between devices  28 us (5%)
  local copies, waits for them, and re-layouts  14.4 us (3%)
  between operations  14.3 us (3%)
  other arithmetic  11.9 us (2%)
    all_to_all x5, waiting for transfers between devices, swap(): lax.all_to_all(rows, 'expert', split_axis=0, concat_axis=0, tiled=True)  241 us
    reduce_scatter x1, waiting for transfers between devices, body(): lax.psum_scatter(outer_dot(arrived, slope).astype(jnp.bfloat16), 'dp', sc...  109 us
    reduce_scatter x1, waiting for transfers between devices, body(): lax.psum_scatter(outer_dot(hidden, upstream).astype(jnp.bfloat16), 'dp',...  99.5 us
    all_to_all x5, starting transfers between devices, swap(): lax.all_to_all(rows, 'expert', split_axis=0, concat_axis=0, tiled=True)  27.7 us
    dot_general x4, matrix products, outer_dot(): lax.dot_general(left, right, (((0,), (0,)), ((), ())), preferred_element_...  15.7 us
  transfers between devices with their start and end apart: 7, of which 7 were waited for; matrix products, arithmetic and copies ran while one was open for 6% of the time, Pallas kernels for 0%

profile of v1, /device:TPU:4, one launch (start us, length us, event | category | flops | bytes accessed | tf_op | source)
XLA Modules:
  0.0 548.8 jit_solution(10603550484338348095)
XLA Ops:
  9.1 2.0 convolution_convert_fusion.3
  11.1 9.1 %all-to-all-start = ((bf16[32,16,2048]{2,1,0:T(8,128)(2,1)}), bf16[32,16,2048]{2,1,0:T(8,128)(2,1)S(1)}, u32[]{:S(2)}, u32[]{:S(2)}) async-start(bf16[32,16,2048]{2,1,0:T(8,128)(2,1)} %bitcast.3), calls=%async_computation | async-start | bytes 4194304 | tf_op jit(solution)/shard_map/all_to_all | solution.py:80
  20.5 2.0 convolution_convert_fusion.2
  22.6 48.0 %all-to-all-done = bf16[32,16,2048]{2,1,0:T(8,128)(2,1)S(1)} async-done(((bf16[32,16,2048]{2,1,0:T(8,128)(2,1)}), bf16[32,16,2048]{2,1,0:T(8,128)(2,1)S(1)}, u32[]{:S(2)}, u32[]{:S(2)}) %all-to-all-start) | async-done | bytes 2097184 | tf_op jit(solution)/shard_map/all_to_all | solution.py:80
  70.6 4.8 all-to-all-start.2
  75.4 4.9 fusion.4
  80.3 45.5 %all-to-all-done.2 = bf16[32,16,2048]{2,1,0:T(8,128)(2,1)} async-done(((bf16[32,16,2048]{2,1,0:T(8,128)(2,1)}), bf16[32,16,2048]{2,1,0:T(8,128)(2,1)}, u32[]{:S(2)}, u32[]{:S(2)}) %all-to-all-start.2) | async-done | bytes 2097184 | tf_op jit(solution)/shard_map/all_to_all | solution.py:80
  125.8 5.6 %convolution_convert_fusion = bf16[768,2048]{1,0:T(8,128)(2,1)} fusion(bf16[512,2048]{1,0:T(8,128)(2,1)} %bitcast.13, f32[512,768]{1,0:T(8,128)} %fusion.4), kind=kOutput, calls=%fused_computation.1 | convolution fusion | flops 1614151680 | bytes 6815744 | tf_op jit(solution)/shard_map/dot_general | solution.py:31
  131.6 8.3 %convolution_convert_fusion.1 = bf16[2048,768]{1,0:T(8,128)(2,1)} fusion(bf16[512,2048]{1,0:T(8,128)(2,1)S(1)} %bitcast.172, f32[512,768]{1,0:T(8,128)} %fusion.4, bf16[512,2048]{1,0:T(8,128)(2,1)} %bitcast.13, bf16[1,768,2048]{2,1,0:T(8,128)(2,1)} %param.19), kind=kOutput, calls=%fused_computation.2 | convolution fusion | flops 3226337280 | bytes 12058624 | tf_op jit(solution)/shard_map/dot_general | solution.py:31
  140.0 99.5 %reduce-scatter.5.cloned.1.call-done = bf16[96,2048]{1,0:T(8,128)(2,1)} async-done(((bf16[768,2048]{1,0:T(8,128)(2,1)}), bf16[96,2048]{1,0:T(8,128)(2,1)}) %reduce-scatter.5.cloned.1.call-update) | async-done | bytes 393232 | tf_op jit(solution)/shard_map/reduce_scatter | solution.py:108
  239.5 1.8 fusion.32
  241.9 109.3 %reduce-scatter.3.cloned.1.call-done = bf16[256,768]{1,0:T(8,128)(2,1)} async-done(((bf16[2048,768]{1,0:T(8,128)(2,1)}), bf16[256,768]{1,0:T(8,128)(2,1)}) %reduce-scatter.3.cloned.1.call-update) | async-done | bytes 393232 | tf_op jit(solution)/shard_map/reduce_scatter | solution.py:111
  351.2 2.6 bitcast_dynamic-update-slice_fusion
  358.3 5.1 all-to-all-start.3
  363.4 5.6 %fusion.6 = bf16[512,2048]{1,0:T(8,128)(2,1)} fusion(bf16[1,768,2048]{2,1,0:T(8,128)(2,1)} %param.19, f32[512,768]{1,0:T(8,128)} %fusion.4), kind=kOutput, calls=%fused_computation.11 | convolution fusion | flops 1613627392 | bytes 6815744 | tf_op jit(solution)/shard_map/dot_general | solution.py:99
  368.9 50.5 %all-to-all-done.3 = bf16[32,288,128]{2,1,0:T(8,128)(2,1)S(1)} async-done(((bf16[32,288,128]{2,1,0:T(8,128)(2,1)}), bf16[32,288,128]{2,1,0:T(8,128)(2,1)S(1)}, u32[]{:S(2)}, u32[]{:S(2)}) %all-to-all-start.3) | async-done | bytes 2359328 | tf_op jit(solution)/shard_map/all_to_all | solution.py:80
  419.4 1.4 copy-done.1
  420.9 4.0 all-to-all-start.1
  425.0 3.9 gather_fusion
  428.9 3.4 broadcast_select_fusion
  432.3 43.0 %all-to-all-done.1 = bf16[32,16,2048]{2,1,0:T(8,128)(2,1)S(1)} async-done(((bf16[32,16,2048]{2,1,0:T(8,128)(2,1)}), bf16[32,16,2048]{2,1,0:T(8,128)(2,1)S(1)}, u32[]{:S(2)}, u32[]{:S(2)}) %all-to-all-start.1) | async-done | bytes 2097184 | tf_op jit(solution)/shard_map/all_to_all | solution.py:80
  475.3 4.8 all-to-all-start.4
  481.9 54.3 %all-to-all-done.4 = bf16[32,288,128]{2,1,0:T(8,128)(2,1)} async-done(((bf16[32,288,128]{2,1,0:T(8,128)(2,1)}), bf16[32,288,128]{2,1,0:T(8,128)(2,1)}, u32[]{:S(2)}, u32[]{:S(2)}) %all-to-all-start.4) | async-done | bytes 2359328 | tf_op jit(solution)/shard_map/all_to_all | solution.py:80
  536.2 2.7 fusion.50
  (59 shorter events, 12.5 us)
Async XLA Ops:
  7.2 1.9 copy-start
  11.1 9.1 %copy-start.8 = (f32[128,2]{0,1:T(2,128)S(1)}, f32[128,2]{0,1:T(2,128)}, u32[]{:S(2)}) copy-start(f32[128,2]{0,1:T(2,128)} %param.14) | copy-start | bytes 3076
  11.1 9.2 %copy-start.5 = (bf16[128,2048]{1,0:T(8,128)(2,1)S(1)}, bf16[128,2048]{1,0:T(8,128)(2,1)}, u32[]{:S(2)}) copy-start(bf16[128,2048]{1,0:T(8,128)(2,1)} %param.15) | copy-start | bytes 1572868
  11.1 59.5 %all-to-all-start = ((bf16[32,16,2048]{2,1,0:T(8,128)(2,1)}), bf16[32,16,2048]{2,1,0:T(8,128)(2,1)S(1)}, u32[]{:S(2)}, u32[]{:S(2)}) async-start(bf16[32,16,2048]{2,1,0:T(8,128)(2,1)} %bitcast.3), calls=%async_computation | async-start | bytes 4194304 | tf_op jit(solution)/shard_map/all_to_all | solution.py:80
  70.6 55.2 %all-to-all-start.2 = ((bf16[32,16,2048]{2,1,0:T(8,128)(2,1)}), bf16[32,16,2048]{2,1,0:T(8,128)(2,1)}, u32[]{:S(2)}, u32[]{:S(2)}) async-start(bf16[32,16,2048]{2,1,0:T(8,128)(2,1)} %bitcast.12), calls=%async_computation.2 | async-start | bytes 4194304 | tf_op jit(solution)/shard_map/all_to_all | solution.py:80
  75.4 164.1 %reduce-scatter.5.cloned.1.call-start = ((), (), s32[]{:S(2)}) async-start(), calls=%async_computation.8 | async-start | bytes 3538944 | tf_op jit(solution)/shard_map/reduce_scatter | solution.py:108
  131.4 219.8 %reduce-scatter.3.cloned.1.call-start = ((), (), s32[]{:S(2)}) async-start(), calls=%async_computation.7 | async-start | bytes 3538944 | tf_op jit(solution)/shard_map/reduce_scatter | solution.py:111
  139.9 99.5 %copy-start.6 = (bf16[1,96,2048]{2,1,0:T(8,128)(2,1)S(1)}, bf16[1,96,2048]{2,1,0:T(8,128)(2,1)}, u32[]{:S(2)}) copy-start(bf16[1,96,2048]{2,1,0:T(8,128)(2,1)} %param.23) | copy-start | bytes 1179652
  139.9 99.5 %copy-start.7 = (bf16[1,96,2048]{2,1,0:T(8,128)(2,1)S(1)}, bf16[1,96,2048]{2,1,0:T(8,128)(2,1)}, u32[]{:S(2)}) copy-start(bf16[1,96,2048]{2,1,0:T(8,128)(2,1)} %param.22) | copy-start | bytes 1179652
  241.4 109.8 %copy-start.3 = (bf16[1,256,768]{2,1,0:T(8,128)(2,1)S(1)}, bf16[1,256,768]{2,1,0:T(8,128)(2,1)}, u32[]{:S(2)}) copy-start(bf16[1,256,768]{2,1,0:T(8,128)(2,1)} %param.20) | copy-start | bytes 1179652
  241.4 109.8 %copy-start.4 = (bf16[1,256,768]{2,1,0:T(8,128)(2,1)S(1)}, bf16[1,256,768]{2,1,0:T(8,128)(2,1)}, u32[]{:S(2)}) copy-start(bf16[1,256,768]{2,1,0:T(8,128)(2,1)} %param.21) | copy-start | bytes 1179652
  351.2 2.6 copy-start.2
  358.3 61.2 %all-to-all-start.3 = ((bf16[32,288,128]{2,1,0:T(8,128)(2,1)}), bf16[32,288,128]{2,1,0:T(8,128)(2,1)S(1)}, u32[]{:S(2)}, u32[]{:S(2)}) async-start(bf16[32,288,128]{2,1,0:T(8,128)(2,1)} %constant_dynamic-update-slice_fusion), calls=%async_computation.5 | async-start | bytes 4718592 | tf_op jit(solution)/shard_map/all_to_all | solution.py:80
  419.4 1.4 copy-start.1
  419.4 5.4 copy-start.9
  419.4 5.4 copy-start.10
  420.9 54.4 %all-to-all-start.1 = ((bf16[32,16,2048]{2,1,0:T(8,128)(2,1)}), bf16[32,16,2048]{2,1,0:T(8,128)(2,1)S(1)}, u32[]{:S(2)}, u32[]{:S(2)}) async-start(bf16[32,16,2048]{2,1,0:T(8,128)(2,1)} %bitcast.173), calls=%async_computation.1 | async-start | bytes 4194304 | tf_op jit(solution)/shard_map/all_to_all | solution.py:80
  475.3 60.9 %all-to-all-start.4 = ((bf16[32,288,128]{2,1,0:T(8,128)(2,1)}), bf16[32,288,128]{2,1,0:T(8,128)(2,1)}, u32[]{:S(2)}, u32[]{:S(2)}) async-start(bf16[32,288,128]{2,1,0:T(8,128)(2,1)} %broadcast_select_fusion), calls=%async_computation.6 | async-start | bytes 4718592 | tf_op jit(solution)/shard_map/all_to_all | solution.py:80
Sparse Core Ops, SparseCore 0:
  131.5 107.8 reduce-scatter.4
  244.2 106.9 reduce-scatter.2

commit v2 on v1

--- a/solution.py
+++ b/solution.py
@@ -1,6 +1,10 @@
+import functools
+
 import jax
 import jax.numpy as jnp
 from jax import lax
+from jax.experimental import pallas as pl
+from jax.experimental.pallas import tpu as pltpu
 from jax.sharding import PartitionSpec as P
 
 beta_one = 0.9
@@ -8,6 +12,9 @@
 adam_eps = 1e-08
 learn_rate = 0.01
 adam_step = 100.0
+n_ring = 4
+n_half = 2
+MESH = pl.DeviceIdType.MESH
 
 
 def silu_slope(preact):
@@ -37,6 +44,298 @@
     return lax.dot_general(
         left, right, (((1,), (1,)), ((), ())), preferred_element_type=jnp.float32
     )
+
+
+def remote(src, dst, send, recv, device):
+    return pltpu.make_async_remote_copy(
+        src_ref=src, dst_ref=dst, send_sem=send, recv_sem=recv, device_id=device, device_id_type=MESH
+    )
+
+
+class Part:
+    def __init__(self, rows, cols, piece):
+        self.rows, self.cols, self.piece = rows, cols, piece
+        self.share = rows // (n_ring * n_half)
+        self.block = rows // n_ring
+        self.side = cols // 2
+        self.per_row = cols // piece[1]
+
+    def where(self, i):
+        r = pl.multiple_of((i // self.per_row) * self.piece[0], 16)
+        c = pl.multiple_of((i % self.per_row) * self.piece[1], 128)
+        return pl.ds(r, self.piece[0]), pl.ds(c, self.piece[1])
+
+    def scratch(self, n_expert):
+        half = (self.block, self.side)
+        return dict(
+            partial=pltpu.VMEM((self.rows, self.cols), jnp.bfloat16),
+            landing=pltpu.VMEM((6,) + half, jnp.bfloat16),
+            relayed=pltpu.VMEM((2,) + half, jnp.bfloat16),
+            own=pltpu.VMEM((self.share, self.cols), jnp.float32),
+            pair_out=pltpu.VMEM((self.share, self.cols), jnp.bfloat16),
+            pair_in=pltpu.VMEM((self.share, self.cols), jnp.bfloat16),
+            stage=pltpu.VMEM((n_expert, 3) + self.piece, jnp.bfloat16),
+            hop_one=pltpu.VMEM((n_expert, 3) + self.piece, jnp.bfloat16),
+            ordered=pltpu.VMEM((n_expert, 3) + self.piece, jnp.bfloat16),
+            hop_two=pltpu.VMEM((n_expert, 3) + self.piece, jnp.bfloat16),
+            ring_send=pltpu.SemaphoreType.DMA((6,)),
+            ring_recv=pltpu.SemaphoreType.DMA((6,)),
+            pair_send=pltpu.SemaphoreType.DMA,
+            pair_recv=pltpu.SemaphoreType.DMA,
+            one_send=pltpu.SemaphoreType.DMA((n_expert,)),
+            one_recv=pltpu.SemaphoreType.DMA((n_expert,)),
+            two_send=pltpu.SemaphoreType.DMA((n_expert,)),
+            two_recv=pltpu.SemaphoreType.DMA((n_expert,)),
+        )
+
+
+part_names = tuple(Part(128, 256, (16, 128)).scratch(32))
+
+
+class Refs:
+    def __init__(self, names, refs):
+        for name, ref in zip(names, refs):
+            setattr(self, name, ref)
+
+
+def finish_kernel(n_expert, parts, *refs):
+    n_in = 18
+    (
+        source_of,
+        slot,
+        gates,
+        produced,
+        tok_t,
+        slope,
+        hid_t,
+        upstream,
+        w_in,
+        m_in,
+        s_in,
+        w_out,
+        m_out,
+        s_out,
+    ) = refs[:14]
+    outs = refs[14:21]
+    mixed = outs[0]
+    returned, back_send, back_recv = refs[21:24]
+    n = len(part_names)
+    pin = Refs(part_names, refs[24 : 24 + n])
+    pout = Refs(part_names, refs[24 + n : 24 + 2 * n])
+    dp = lax.axis_index("dp")
+    me = lax.axis_index("expert")
+    x, zh = dp // 2, dp % 2
+    ahead, behind, across = (x + 1) % 4, (x + 3) % 4, (x + 2) % 4
+    to_ahead = (ahead * 2 + zh, me)
+    to_behind = (behind * 2 + zh, me)
+    to_pair = (x * 2 + 1 - zh, me)
+    peers = n_expert - 1
+
+    def peer(j):
+        return (me + j) % n_expert
+
+    barrier = pltpu.get_barrier_semaphore()
+
+    @pl.loop(1, n_expert)
+    def _(j):
+        pl.semaphore_signal(barrier, inc=1, device_id=(dp, peer(j)), device_id_type=MESH)
+
+    for device in (to_ahead, to_behind, to_pair):
+        pl.semaphore_signal(barrier, inc=1, device_id=device, device_id_type=MESH)
+    pl.semaphore_wait(barrier, peers + 3)
+
+    def all_send(src, dst, send, recv):
+        @pl.loop(1, n_expert)
+        def _(j):
+            d = peer(j)
+            remote(src.at[d], dst.at[me], send.at[d], recv.at[me], (dp, d)).start()
+
+        dst[me] = src[me]
+
+    def all_recv(src, dst, send, recv):
+        @pl.loop(1, n_expert)
+        def _(j):
+            d = peer(j)
+            remote(src.at[d], dst.at[d], send.at[d], recv.at[d], (dp, d)).wait_recv()
+
+    def all_sent(src, dst, send, recv):
+        @pl.loop(1, n_expert)
+        def _(j):
+            d = peer(j)
+            remote(src.at[d], dst.at[d], send.at[d], recv.at[d], (dp, d)).wait_send()
+
+    def ring_copies(p, part):
+        def side(block, half):
+            r = pl.multiple_of(block * part.block, 16)
+            return p.partial.at[pl.ds(r, part.block), pl.ds(half * part.side, part.side)]
+
+        plan = [
+            (side(across, 0), 0, to_ahead),
+            (side(across, 1), 1, to_behind),
+            (side(ahead, 1), 2, to_ahead),
+            (side(behind, 0), 3, to_behind),
+            (p.relayed.at[0], 4, to_ahead),
+            (p.relayed.at[1], 5, to_behind),
+        ]
+        def copy(k):
+            src, slot_of, device = plan[k]
+            return remote(
+                src, p.landing.at[slot_of], p.ring_send.at[k], p.ring_recv.at[k], device
+            )
+
+        return copy
+
+    def ring_first(p, part, left, right):
+        def fill(block):
+            step = min(part.block, 256)
+            base = block * part.block
+
+            @pl.loop(0, part.block // step)
+            def _(i):
+                r = pl.ds(pl.multiple_of(base + i * step, 16), step)
+                p.partial[r, :] = jnp.dot(
+                    left[r, :], right[...], preferred_element_type=jnp.float32
+                ).astype(jnp.bfloat16)
+
+        copies = ring_copies(p, part)
+        fill(across)
+        copies(0).start()
+        copies(1).start()
+        fill(ahead)
+        copies(2).start()
+        fill(behind)
+        copies(3).start()
+        fill(x)
+
+    def ring_second(p, part):
+        copies = ring_copies(p, part)
+        for k, block in ((0, ahead), (1, behind)):
+            copies(k).wait_recv()
+
+            @pl.loop(0, part.block // 16)
+            def _(i):
+                r = pl.ds(pl.multiple_of(i * 16, 16), 16)
+                q = pl.ds(pl.multiple_of(block * part.block + i * 16, 16), 16)
+                mine = p.partial[q, pl.ds(k * part.side, part.side)].astype(jnp.float32)
+                p.relayed[k, r, :] = (p.landing[k, r, :].astype(jnp.float32) + mine).astype(
+                    jnp.bfloat16
+                )
+
+            copies(4 + k).start()
+
+    def pair_copy(p):
+        return remote(p.pair_out, p.pair_in, p.pair_send, p.pair_recv, to_pair)
+
+    def ring_third(p, part):
+        copies = ring_copies(p, part)
+        for k in (2, 3, 4, 5):
+            copies(k).wait_recv()
+
+        def total(half, base, i, k):
+            r = pl.ds(pl.multiple_of(base + i * 16, 16), 16)
+            q = pl.ds(pl.multiple_of(x * part.block + base + i * 16, 16), 16)
+            mine = p.partial[q, pl.ds(half * part.side, part.side)].astype(jnp.float32)
+            return (
+                mine
+                + p.landing[4 + half, r, :].astype(jnp.float32)
+                + p.landing[3 - half, r, :].astype(jnp.float32)
+            )
+
+        @pl.loop(0, part.share // 16)
+        def _(i):
+            q = pl.ds(pl.multiple_of(i * 16, 16), 16)
+            for half in range(2):
+                p.pair_out[q, pl.ds(half * part.side, part.side)] = total(
+                    half, (1 - zh) * part.share, i, 0
+                ).astype(jnp.bfloat16)
+
+        pair_copy(p).start()
+
+        @pl.loop(0, part.share // 16)
+        def _(i):
+            q = pl.ds(pl.multiple_of(i * 16, 16), 16)
+            for half in range(2):
+                p.own[q, pl.ds(half * part.side, part.side)] = total(half, zh * part.share, i, 0)
+
+    def hop_first(p, part, weight, mean, square):
+        pair_copy(p).wait_recv()
+
+        def piece(i):
+            at = part.where(i)
+            gradient = p.own[at] + p.pair_in[at].astype(jnp.float32)
+            after = adam_apply(weight[at], mean[at], square[at], gradient)
+            for k in range(3):
+                p.stage[i, k] = after[k]
+
+        @pl.loop(1, n_expert)
+        def _(j):
+            d = peer(j)
+            piece(d)
+            remote(
+                p.stage.at[d], p.hop_one.at[me], p.one_send.at[d], p.one_recv.at[me], (dp, d)
+            ).start()
+
+        piece(me)
+        p.hop_one[me] = p.stage[me]
+
+    def hop_second(p, part):
+        all_recv(p.stage, p.hop_one, p.one_send, p.one_recv)
+
+        @pl.loop(1, n_expert)
+        def _(j):
+            d = peer(j)
+            p.ordered[d] = p.hop_one[source_of[d]]
+            remote(
+                p.ordered.at[d], p.hop_two.at[me], p.two_send.at[d], p.two_recv.at[me], (dp, d)
+            ).start()
+
+        p.hop_two[me] = p.hop_one[source_of[me]]
+
+    def arrive(p, part, results):
+        all_recv(p.ordered, p.hop_two, p.two_send, p.two_recv)
+
+        @pl.loop(0, n_expert)
+        def _(i):
+            at = part.where(i)
+            for k in range(3):
+                results[k][at] = p.hop_two[i, k]
+
+    def mix():
+        all_recv(produced, returned, back_send, back_recv)
+        tok_rows = slot.shape[0]
+        width = produced.shape[2]
+        cap = produced.shape[1]
+        back = returned[...].reshape(n_expert * cap, width)
+        lanes = lax.broadcasted_iota(jnp.int32, (tok_rows, n_expert * cap), 1)
+        total = None
+        for k in range(2):
+            pick = (slot[:, k : k + 1] == lanes).astype(jnp.float32).astype(jnp.bfloat16)
+            term = gates[:, k : k + 1] * jnp.dot(pick, back, preferred_element_type=jnp.float32)
+            total = term if total is None else total + term
+        mixed[...] = total.astype(jnp.bfloat16)
+
+    part_in, part_out = parts
+    ring_first(pout, part_out, hid_t, upstream)
+    all_send(produced, returned, back_send, back_recv)
+    ring_first(pin, part_in, tok_t, slope)
+    ring_second(pout, part_out)
+    ring_second(pin, part_in)
+    ring_third(pout, part_out)
+    ring_third(pin, part_in)
+    mix()
+    hop_first(pout, part_out, w_out, m_out, s_out)
+    hop_first(pin, part_in, w_in, m_in, s_in)
+    hop_second(pout, part_out)
+    hop_second(pin, part_in)
+    arrive(pout, part_out, outs[4:7])
+    arrive(pin, part_in, outs[1:4])
+    all_sent(produced, returned, back_send, back_recv)
+    for p, part in ((pout, part_out), (pin, part_in)):
+        for k in range(6):
+            ring_copies(p, part)(k).wait_send()
+        pair_copy(p).wait_send()
+        all_sent(p.stage, p.hop_one, p.one_send, p.one_recv)
+        all_sent(p.ordered, p.hop_two, p.two_send, p.two_recv)
 
 
 def body(
@@ -99,59 +398,54 @@
     produced = jnp.dot(hidden, weight_out[0], preferred_element_type=jnp.float32).astype(
         jnp.bfloat16
     )
-    returned = exchange(produced)
-    mixed = sum(
-        route_gates[:, k, None] * outer_dot(place[k], returned) for k in range(picks_each)
-    ).astype(jnp.bfloat16)
     downward = right_dot(upstream, weight_out[0])
     slope = (downward * silu_slope(preact)).astype(jnp.bfloat16)
-    grad_out = lax.psum_scatter(
-        outer_dot(hidden, upstream).astype(jnp.bfloat16), "dp", scatter_dimension=0, tiled=True
-    ).astype(jnp.float32)
-    grad_in = lax.psum_scatter(
-        outer_dot(arrived, slope).astype(jnp.bfloat16), "dp", scatter_dimension=0, tiled=True
-    ).astype(jnp.float32)
     in_share = lax.dynamic_slice_in_dim(weight_in[0], group * rows_in, rows_in, 0)
     out_share = lax.dynamic_slice_in_dim(weight_out[0], group * rows_out, rows_out, 0)
-    after_in = adam_apply(in_share, mean_in[0], square_in[0], grad_in)
-    after_out = adam_apply(out_share, mean_out[0], square_out[0], grad_out)
-    lanes = 128
-    deep = rows_in // n_expert
-    wide = hidden_width // lanes
-    tall = rows_out // 2
-    cols = width // lanes
-
-    def pieces_in(share):
-        cut = share.reshape(n_expert, deep, wide, lanes).transpose(0, 2, 1, 3)
-        return cut.reshape(n_expert, wide * deep, lanes)
-
-    def joined_in(cut):
-        share = cut.reshape(n_expert, wide, deep, lanes).transpose(0, 2, 1, 3)
-        return share.reshape(1, rows_in, hidden_width)
-
-    def pieces_out(share):
-        cut = share.reshape(2, tall, cols, lanes).transpose(0, 2, 1, 3)
-        return cut.reshape(n_expert, tall, lanes)
-
-    def joined_out(cut):
-        share = cut.reshape(2, cols, tall, lanes).transpose(0, 2, 1, 3)
-        return share.reshape(1, rows_out, width)
-
-    packed = jnp.concatenate(
-        [pieces_in(part) for part in after_in] + [pieces_out(part) for part in after_out], axis=1
-    )
-    spread = swap(packed)
-    landed = swap(jnp.take(spread, source_of, axis=0))
-    moved = jnp.split(landed, 6, axis=1)
-    return (
-        mixed,
-        joined_in(moved[0]),
-        joined_in(moved[1]),
-        joined_in(moved[2]),
-        joined_out(moved[3]),
-        joined_out(moved[4]),
-        joined_out(moved[5]),
-    )
+
+    parts = (
+        Part(width, hidden_width, (16, hidden_width // 2)),
+        Part(hidden_width, width, (rows_out // 2, 128)),
+    )
+    vmem = pl.BlockSpec(memory_space=pltpu.VMEM)
+    smem = pl.BlockSpec(memory_space=pltpu.SMEM)
+    shares_in = jax.ShapeDtypeStruct((rows_in, hidden_width), jnp.bfloat16)
+    shares_out = jax.ShapeDtypeStruct((rows_out, width), jnp.bfloat16)
+    results = pl.pallas_call(
+        functools.partial(finish_kernel, n_expert, parts),
+        out_shape=[jax.ShapeDtypeStruct((tok_rows, width), jnp.bfloat16)]
+        + [shares_in] * 3
+        + [shares_out] * 3,
+        in_specs=[smem] + [vmem] * 13,
+        out_specs=[vmem] * 7,
+        scratch_shapes=[
+            pltpu.VMEM((n_expert, capacity, width), jnp.bfloat16),
+            pltpu.SemaphoreType.DMA((n_expert,)),
+            pltpu.SemaphoreType.DMA((n_expert,)),
+        ]
+        + list(parts[0].scratch(n_expert).values())
+        + list(parts[1].scratch(n_expert).values()),
+        compiler_params=pltpu.CompilerParams(
+            collective_id=0, has_side_effects=True, vmem_limit_bytes=60 << 20
+        ),
+        name="finish",
+    )(
+        source_of,
+        slot,
+        route_gates,
+        produced.reshape(n_expert, capacity, width),
+        arrived.T,
+        slope,
+        hidden.T,
+        upstream,
+        in_share,
+        mean_in[0],
+        square_in[0],
+        out_share,
+        mean_out[0],
+        square_out[0],
+    )
+    return (results[0],) + tuple(piece[None] for piece in results[1:])
 
 
 def solution(mesh):

time: 551 us -> 337 us (0.61)
  waiting for transfers between devices: 450 us -> 76.2 us
  Pallas kernels: 0 us -> 198 us
  starting transfers between devices: 28 us -> 14.3 us
  between operations: 14.3 us -> 0.78 us
  matrix products: 30.2 us -> 20.3 us
  other arithmetic: 11.9 us -> 5.06 us
    reduce_scatter x2 -> x0, waiting for transfers between devices: 209 us -> none  [the longest x1 109 us: body(): lax.psum_scatter(outer_dot(arrived, slope).astype(jnp.bfloat16), 'dp', sc...]
    pallas_call x0 -> x1, Pallas kernels: none -> 198 us  [body(): pl.pallas_call(functools.partial(finish_kernel, n_expert, parts), out_sha...]
    all_to_all x5 -> x2, waiting for transfers between devices: 241 us -> 76.2 us  [swap(): lax.all_to_all(rows, 'expert', split_axis=0, concat_axis=0, tiled=True)]
    all_to_all x5 -> x2, starting transfers between devices: 27.7 us -> 14.3 us  [swap(): lax.all_to_all(rows, 'expert', split_axis=0, concat_axis=0, tiled=True)]
    dot_general x4 -> x1, matrix products: 15.7 us -> 5.09 us  [right_dot(): lax.dot_general(left, right, (((1,), (1,)), ((), ())), preferred_element_...]
    unnamed x4 -> x0, other arithmetic: 6.35 us -> none
  transfers between devices with their start and end apart: 7 -> 2, of which waited for: 7 -> 2; matrix products, arithmetic and copies ran while one was open for 6% -> 7% of each run, Pallas kernels for 0% -> 0%
where the time goes in v2:
time: 337 us; the launch traced here: 333 us
  Pallas kernels  198 us (59%)
  waiting for transfers between devices  76.2 us (23%)
  matrix products  20.3 us (6%)
  local copies, waits for them, and re-layouts  18.4 us (5%)
  starting transfers between devices  14.3 us (4%)
  other arithmetic  5.06 us (2%)
    pallas_call x1, Pallas kernels, body(): pl.pallas_call(functools.partial(finish_kernel, n_expert, parts), out_sha...  198 us
    all_to_all x2, waiting for transfers between devices, swap(): lax.all_to_all(rows, 'expert', split_axis=0, concat_axis=0, tiled=True)  76.2 us
    all_to_all x2, starting transfers between devices, swap(): lax.all_to_all(rows, 'expert', split_axis=0, concat_axis=0, tiled=True)  14.3 us
    unnamed x30, local copies, waits for them, and re-layouts  8.33 us
  transfers between devices with their start and end apart: 2, of which 2 were waited for; matrix products, arithmetic and copies ran while one was open for 7% of the time, Pallas kernels for 0%

profile of v2, /device:TPU:4, one launch (start us, length us, event | category | flops | bytes accessed | tf_op | source)
XLA Modules:
  0.0 332.7 jit_solution(1257894432903739262)
XLA Ops:
  0.6 0.8 convert_reduce_fusion
  1.8 0.8 select_reduce_fusion
  3.1 3.1 convolution_convert_fusion.1
  6.2 9.2 %all-to-all-start = ((bf16[32,16,2048]{2,1,0:T(8,128)(2,1)}), bf16[32,16,2048]{2,1,0:T(8,128)(2,1)}, u32[]{:S(2)}, u32[]{:S(2)}) async-start(bf16[32,16,2048]{2,1,0:T(8,128)(2,1)} %bitcast.53), calls=%async_computation | async-start | bytes 4194304 | tf_op jit(solution)/shard_map/all_to_all | solution.py:379
  15.4 1.3 fusion.15
  16.7 2.1 convolution_convert_fusion
  18.8 47.0 %all-to-all-done = bf16[32,16,2048]{2,1,0:T(8,128)(2,1)} async-done(((bf16[32,16,2048]{2,1,0:T(8,128)(2,1)}), bf16[32,16,2048]{2,1,0:T(8,128)(2,1)}, u32[]{:S(2)}, u32[]{:S(2)}) %all-to-all-start) | async-done | bytes 2097184 | tf_op jit(solution)/shard_map/all_to_all | solution.py:379
  65.8 5.1 %all-to-all-start.1 = ((bf16[32,16,2048]{2,1,0:T(8,128)(2,1)}), bf16[32,16,2048]{2,1,0:T(8,128)(2,1)}, u32[]{:S(2)}, u32[]{:S(2)}) async-start(bf16[32,16,2048]{2,1,0:T(8,128)(2,1)} %bitcast.52), calls=%async_computation.1 | async-start | bytes 4194304 | tf_op jit(solution)/shard_map/all_to_all | solution.py:379
  72.2 1.8 dynamic-slice_bitcast_fusion.1.refs_8_
  74.0 0.8 dynamic-slice_bitcast_fusion.refs_11_
  74.7 3.9 %copy.41 = bf16[512,2048]{0,1:T(8,128)(2,1)} copy(bf16[512,2048]{1,0:T(8,128)(2,1)} %bitcast.1) | data formatting | bytes 4194304 | tf_op jit(solution)/shard_map/reshape | solution.py:382
  78.7 5.5 %fusion.4 = f32[512,768]{1,0:T(8,128)} fusion(bf16[512,2048]{1,0:T(8,128)(2,1)} %bitcast.1, bf16[1,2048,768]{2,1,0:T(8,128)(2,1)} %param.18), kind=kOutput, calls=%fused_computation.4 | convolution fusion | flops 1610612736 | bytes 6815744 | tf_op jit(solution)/shard_map/dot_general | solution.py:396
  84.2 3.0 copy.42
  87.3 4.5 %fusion.6 = bf16[512,2048]{1,0:T(8,128)(2,1)} fusion(bf16[1,768,2048]{2,1,0:T(8,128)(2,1)S(1)} %copy-done, f32[512,768]{1,0:T(8,128)} %fusion.4), kind=kOutput, calls=%fused_computation.8 | convolution fusion | flops 1613627392 | bytes 6815744 | tf_op jit(solution)/shard_map/dot_general | solution.py:398
  91.8 29.3 %all-to-all-done.1 = bf16[32,16,2048]{2,1,0:T(8,128)(2,1)} async-done(((bf16[32,16,2048]{2,1,0:T(8,128)(2,1)}), bf16[32,16,2048]{2,1,0:T(8,128)(2,1)}, u32[]{:S(2)}, u32[]{:S(2)}) %all-to-all-start.1) | async-done | bytes 2097184 | tf_op jit(solution)/shard_map/all_to_all | solution.py:379
  121.1 5.1 %multiply_convert_fusion.refs_5_ = bf16[512,768]{1,0:T(8,128)(2,1)} fusion(f32[512,768]{1,0:T(8,128)} %fusion.4, bf16[512,2048]{1,0:T(8,128)(2,1)} %bitcast.9.refs_7_, bf16[1,768,2048]{2,1,0:T(8,128)(2,1)S(1)} %copy-done), kind=kOutput, calls=%fused_computation.14 | convolution fusion | flops 1614151680 | bytes 7602176 | tf_op jit(solution)/shard_map/dot_general | solution.py:44
  126.2 1.3 fusion.12.refs_6_
  127.5 197.7 %finish.1 = (bf16[128,2048]{1,0:T(8,128)(2,1)}, bf16[256,768]{1,0:T(8,128)(2,1)}, bf16[256,768]{1,0:T(8,128)(2,1)}, bf16[256,768]{1,0:T(8,128)(2,1)}, bf16[96,20...) custom-call(s32[32]{0:T(128)} %select_reduce_fusion.2.refs_0_, s32[128,2]{1,0:T(8,128)} %copy-done.2, ...), custom_call_target="tpu_custom_call" | custom-call | tf_op jit(solution)/shard_map/finish/pallas_call | solution.py:414
  325.2 2.0 copy.51
  327.2 1.8 copy.52
  329.0 0.7 copy.53
  329.7 0.7 copy.54
  330.5 0.7 copy.55
  332.0 0.7 copy.57
  (36 shorter events, 3.0 us)
Async XLA Ops:
  0.6 73.3 %copy-start = (bf16[1,768,2048]{2,1,0:T(8,128)(2,1)S(1)}, bf16[1,768,2048]{2,1,0:T(8,128)(2,1)}, u32[]{:S(2)}) copy-start(bf16[1,768,2048]{2,1,0:T(8,128)(2,1)} %param.19) | copy-start | bytes 9437188
  2.9 3.3 copy-start.2
  6.2 9.2 %copy-start.8 = (f32[128,2]{0,1:T(2,128)S(1)}, f32[128,2]{0,1:T(2,128)}, u32[]{:S(2)}) copy-start(f32[128,2]{0,1:T(2,128)} %param.14) | copy-start | bytes 3076
  6.2 59.6 %all-to-all-start = ((bf16[32,16,2048]{2,1,0:T(8,128)(2,1)}), bf16[32,16,2048]{2,1,0:T(8,128)(2,1)}, u32[]{:S(2)}, u32[]{:S(2)}) async-start(bf16[32,16,2048]{2,1,0:T(8,128)(2,1)} %bitcast.53), calls=%async_computation | async-start | bytes 4194304 | tf_op jit(solution)/shard_map/all_to_all | solution.py:379
  65.8 5.8 %copy-start.9 = (s32[32]{0:T(128)S(1)}, s32[32]{0:T(128)}, u32[]{:S(2)}) copy-start(s32[32]{0:T(128)} %param.16) | copy-start | bytes 388
  65.8 5.8 %copy-start.10 = (s32[32]{0:T(128)S(1)}, s32[32]{0:T(128)}, u32[]{:S(2)}) copy-start(s32[32]{0:T(128)} %param.17) | copy-start | bytes 388
  65.8 55.3 %all-to-all-start.1 = ((bf16[32,16,2048]{2,1,0:T(8,128)(2,1)}), bf16[32,16,2048]{2,1,0:T(8,128)(2,1)}, u32[]{:S(2)}, u32[]{:S(2)}) async-start(bf16[32,16,2048]{2,1,0:T(8,128)(2,1)} %bitcast.52), calls=%async_computation.1 | async-start | bytes 4194304 | tf_op jit(solution)/shard_map/all_to_all | solution.py:379
  121.1 5.1 %copy-start.1 = (f32[512,768]{0,1:T(8,128)S(1)}, f32[512,768]{0,1:T(8,128)}, u32[]{:S(2)}) copy-start(f32[512,768]{0,1:T(8,128)} %copy.42) | copy-start | bytes 4718596
  325.1 3.9 %copy-start.7 = (bf16[256,768]{1,0:T(8,128)(2,1)S(1)}, bf16[256,768]{1,0:T(8,128)(2,1)}, u32[]{:S(2)}) copy-start(bf16[256,768]{1,0:T(8,128)(2,1)} %get-tuple-element.16) | copy-start | bytes 1179652
  325.1 4.6 %copy-start.6 = (bf16[256,768]{1,0:T(8,128)(2,1)S(1)}, bf16[256,768]{1,0:T(8,128)(2,1)}, u32[]{:S(2)}) copy-start(bf16[256,768]{1,0:T(8,128)(2,1)} %get-tuple-element.17) | copy-start | bytes 1179652
  325.2 5.3 %copy-start.5 = (bf16[96,2048]{1,0:T(8,128)(2,1)S(1)}, bf16[96,2048]{1,0:T(8,128)(2,1)}, u32[]{:S(2)}) copy-start(bf16[96,2048]{1,0:T(8,128)(2,1)} %get-tuple-element.18) | copy-start | bytes 1179652
  325.2 6.1 %copy-start.4 = (bf16[96,2048]{1,0:T(8,128)(2,1)S(1)}, bf16[96,2048]{1,0:T(8,128)(2,1)}, u32[]{:S(2)}) copy-start(bf16[96,2048]{1,0:T(8,128)(2,1)} %get-tuple-element.19) | copy-start | bytes 1179652
  327.2 4.8 %copy-start.3 = (bf16[96,2048]{1,0:T(8,128)(2,1)S(1)}, bf16[96,2048]{1,0:T(8,128)(2,1)}, u32[]{:S(2)}) copy-start(bf16[96,2048]{1,0:T(8,128)(2,1)} %get-tuple-element.20) | copy-start | bytes 1179652

commit v3 on v2

--- a/solution.py
+++ b/solution.py
@@ -76,8 +76,11 @@
             pair_in=pltpu.VMEM((self.share, self.cols), jnp.bfloat16),
             stage=pltpu.VMEM((n_expert, 3) + self.piece, jnp.bfloat16),
             hop_one=pltpu.VMEM((n_expert, 3) + self.piece, jnp.bfloat16),
-            ordered=pltpu.VMEM((n_expert, 3) + self.piece, jnp.bfloat16),
             hop_two=pltpu.VMEM((n_expert, 3) + self.piece, jnp.bfloat16),
+            weight=pltpu.VMEM((self.rows, self.cols), jnp.bfloat16),
+            mean=pltpu.VMEM((self.share, self.cols), jnp.bfloat16),
+            square=pltpu.VMEM((self.share, self.cols), jnp.bfloat16),
+            load=pltpu.SemaphoreType.DMA((3,)),
             ring_send=pltpu.SemaphoreType.DMA((6,)),
             ring_recv=pltpu.SemaphoreType.DMA((6,)),
             pair_send=pltpu.SemaphoreType.DMA,
@@ -90,6 +93,44 @@
 
 
 part_names = tuple(Part(128, 256, (16, 128)).scratch(32))
+n_line = 4
+n_plane = 8
+
+
+def flow_scratch(rows, cap, width):
+    return dict(
+        raw=pltpu.VMEM((n_line, rows, width), jnp.bfloat16),
+        sent=pltpu.VMEM((n_line, n_plane, cap, width), jnp.bfloat16),
+        came=pltpu.VMEM((n_line, n_plane, cap, width), jnp.bfloat16),
+        load=pltpu.SemaphoreType.DMA,
+        z_send=pltpu.SemaphoreType.DMA((2, n_line)),
+        z_recv=pltpu.SemaphoreType.DMA((n_line,)),
+        y_send=pltpu.SemaphoreType.DMA((n_line, n_plane)),
+        y_recv=pltpu.SemaphoreType.DMA((n_line, n_plane)),
+    )
+
+
+flow_names = tuple(flow_scratch(128, 16, 2048))
+
+
+def other_scratch(rows, cap, width, hidden, n_expert):
+    slots = n_expert * cap
+    return dict(
+        meta=pltpu.VMEM((n_line, 8, rows), jnp.float32),
+        meta_send=pltpu.SemaphoreType.DMA((2, n_line)),
+        meta_recv=pltpu.SemaphoreType.DMA((n_line,)),
+        table=pltpu.VMEM((rows, 128), jnp.float32),
+        preact=pltpu.VMEM((slots, hidden), jnp.float32),
+        hid_t=pltpu.VMEM((hidden, slots), jnp.bfloat16),
+        tok_t=pltpu.VMEM((width, slots), jnp.bfloat16),
+        slope=pltpu.VMEM((slots, hidden), jnp.bfloat16),
+        returned=pltpu.VMEM((n_expert, cap, width), jnp.bfloat16),
+        back_send=pltpu.SemaphoreType.DMA((n_expert,)),
+        back_recv=pltpu.SemaphoreType.DMA((n_expert,)),
+    )
+
+
+other_names = tuple(other_scratch(128, 16, 2048, 768, 32))
 
 
 class Refs:
@@ -98,30 +139,37 @@
             setattr(self, name, ref)
 
 
-def finish_kernel(n_expert, parts, *refs):
-    n_in = 18
+def whole_kernel(n_expert, parts, *refs):
     (
         source_of,
-        slot,
+        owner,
+        route_ids,
         gates,
-        produced,
-        tok_t,
-        slope,
-        hid_t,
-        upstream,
+        tokens,
+        cotangent,
         w_in,
         m_in,
         s_in,
         w_out,
         m_out,
         s_out,
-    ) = refs[:14]
-    outs = refs[14:21]
+    ) = refs[:12]
+    outs = refs[12:19]
     mixed = outs[0]
-    returned, back_send, back_recv = refs[21:24]
-    n = len(part_names)
-    pin = Refs(part_names, refs[24 : 24 + n])
-    pout = Refs(part_names, refs[24 + n : 24 + 2 * n])
+    rest = list(refs[19:])
+
+    def take(names):
+        group = Refs(names, rest[: len(names)])
+        del rest[: len(names)]
+        return group
+
+    tok, cot = take(flow_names), take(flow_names)
+    sc = take(other_names)
+    pin, pout = take(part_names), take(part_names)
+    part_in, part_out = parts
+    rows, width = mixed.shape
+    cap = sc.returned.shape[1]
+    slots = n_expert * cap
     dp = lax.axis_index("dp")
     me = lax.axis_index("expert")
     x, zh = dp // 2, dp % 2
@@ -130,9 +178,27 @@
     to_behind = (behind * 2 + zh, me)
     to_pair = (x * 2 + 1 - zh, me)
     peers = n_expert - 1
+    zl = (me // 2) % n_line
+    mine = (me // 8) * 2 + me % 2
 
     def peer(j):
         return (me + j) % n_expert
+
+    def loads():
+        plan = [
+            (tokens, tok.raw.at[zl], tok.load),
+            (cotangent, cot.raw.at[zl], cot.load),
+        ]
+        for p, sources in ((pin, (w_in, m_in, s_in)), (pout, (w_out, m_out, s_out))):
+            for k, target in enumerate((p.weight, p.mean, p.square)):
+                plan.append((sources[k], target, p.load.at[k]))
+        return plan
+
+    def load(k):
+        return pltpu.make_async_copy(*loads()[k])
+
+    for k in range(8):
+        load(k).start()
 
     barrier = pltpu.get_barrier_semaphore()
 
@@ -142,27 +208,200 @@
 
     for device in (to_ahead, to_behind, to_pair):
         pl.semaphore_signal(barrier, inc=1, device_id=device, device_id_type=MESH)
+
+    def place_own():
+        lanes = lax.broadcasted_iota(jnp.int32, (rows, n_expert), 1)
+        picked = [(route_ids[:, k : k + 1] == lanes).astype(jnp.float32) for k in range(2)]
+        earlier = (
+            lax.broadcasted_iota(jnp.int32, (rows, rows), 1)
+            < lax.broadcasted_iota(jnp.int32, (rows, rows), 0)
+        ).astype(jnp.float32)
+        before = jnp.dot(
+            earlier.astype(jnp.bfloat16),
+            (picked[0] + picked[1]).astype(jnp.bfloat16),
+            preferred_element_type=jnp.float32,
+        )
+        held = owner[...].astype(jnp.float32) * float(cap)
+        slot = [jnp.sum(one * (before + held), axis=1, keepdims=True) for one in picked]
+        lane = lax.broadcasted_iota(jnp.int32, (rows, 128), 1)
+        table = jnp.where(
+            lane == 0,
+            slot[0],
+            jnp.where(lane == 1, slot[1], jnp.where(lane == 2, gates[:, 0:1], gates[:, 1:2])),
+        )
+        sc.table[...] = table
+        sc.meta[zl] = table.T[0:8, :]
+
+    place_own()
     pl.semaphore_wait(barrier, peers + 3)
 
-    def all_send(src, dst, send, recv):
+    def z_copies(buf, send, recv, direction, block):
+        neighbour = (dp, me + 2 if direction == 0 else me - 2)
+        return remote(
+            buf.at[block], buf.at[block], send.at[direction, block], recv.at[block], neighbour
+        )
+
+    def z_send(flow, direction, block):
+        z_copies(flow.raw, flow.z_send, flow.z_recv, direction, block).start()
+        if flow is tok:
+            z_copies(sc.meta, sc.meta_send, sc.meta_recv, direction, block).start()
+
+    def z_wait(flow, direction, block, sent):
+        copy = z_copies(flow.raw, flow.z_send, flow.z_recv, direction, block)
+        copy.wait_send() if sent else copy.wait_recv()
+        if flow is tok:
+            copy = z_copies(sc.meta, sc.meta_send, sc.meta_recv, direction, block)
+            copy.wait_send() if sent else copy.wait_recv()
+
+    def z_first(flow):
+        pl.when(zl < n_line - 1)(lambda: z_send(flow, 0, zl))
+        pl.when(zl > 0)(lambda: z_send(flow, 1, zl))
+
+    def z_step(flow, step):
+        left, right = zl - 1 - step, zl + 1 + step
+
+        @pl.when(left >= 0)
+        def _():
+            z_wait(flow, 0, left, False)
+            pl.when(zl < n_line - 1)(lambda: z_send(flow, 0, left))
+
+        @pl.when(right < n_line)
+        def _():
+            z_wait(flow, 1, right, False)
+            pl.when(zl > 0)(lambda: z_send(flow, 1, right))
+
+    def z_sent(flow):
+        @pl.loop(0, n_line)
+        def _(block):
+            pl.when((zl < n_line - 1) & (block <= zl))(lambda: z_wait(flow, 0, block, True))
+            pl.when((zl > 0) & (block >= zl))(lambda: z_wait(flow, 1, block, True))
+
+    def y_copy(flow, block, q):
+        device = (dp, (q // 2) * 8 + zl * 2 + q % 2)
+        return remote(
+            flow.sent.at[block, q],
+            flow.came.at[block, mine],
+            flow.y_send.at[block, q],
+            flow.y_recv.at[block, mine],
+            device,
+        )
+
+    def y_got(flow, block, q):
+        device = (dp, (q // 2) * 8 + zl * 2 + q % 2)
+        return remote(
+            flow.sent.at[block, q],
+            flow.came.at[block, q],
+            flow.y_send.at[block, q],
+            flow.y_recv.at[block, q],
+            device,
+        )
+
+    def y_send(flow, block):
+        r = lax.broadcasted_iota(jnp.int32, (n_plane * cap, rows), 0)
+        here = ((r // (2 * cap)) * (n_expert * cap // 4) + r % (2 * cap) + zl * (2 * cap)).astype(
+            jnp.float32
+        )
+        pick = [
+            (sc.meta[block, k : k + 1, :] == here).astype(jnp.float32).astype(jnp.bfloat16)
+            for k in range(2)
+        ]
+        if flow is tok:
+            put = jnp.dot(pick[0] + pick[1], flow.raw[block], preferred_element_type=jnp.float32)
+        else:
+            put = None
+            for k in range(2):
+                gate = jnp.broadcast_to(sc.meta[block, 2 + k : 3 + k, :], (rows, rows)).T[:, 0:1]
+                scaled = (gate * flow.raw[block].astype(jnp.float32)).astype(jnp.bfloat16)
+                term = jnp.dot(pick[k], scaled, preferred_element_type=jnp.float32)
+                put = term if put is None else put + term
+        flow.sent[block] = put.astype(jnp.bfloat16).reshape(n_plane, cap, width)
+
+        @pl.loop(1, n_plane)
+        def _(j):
+            y_copy(flow, block, (mine + j) % n_plane).start()
+
+        flow.came[block, mine] = flow.sent[block, mine]
+
+    def y_step(flow, step):
+        left, right = zl - 1 - step, zl + 1 + step
+        pl.when(left >= 0)(lambda: y_send(flow, left))
+        pl.when(right < n_line)(lambda: y_send(flow, right))
+
+    def y_all(flow, sent):
+        @pl.loop(0, n_line)
+        def _(block):
+            @pl.loop(1, n_plane)
+            def _(j):
+                q = (mine + j) % n_plane
+                if sent:
+                    y_copy(flow, block, q).wait_send()
+                else:
+                    y_got(flow, block, q).wait_recv()
+
+    def forward():
+        y_all(tok, False)
+        y_all(tok, True)
+        step = n_plane * cap
+
+        @pl.loop(0, n_line)
+        def _(i):
+            r = pl.ds(pl.multiple_of(i * step, step), step)
+            preact = jnp.dot(
+                tok.came[i].reshape(step, width), pin.weight[...], preferred_element_type=jnp.float32
+            )
+            sc.preact[r, :] = preact
+            hidden = jax.nn.silu(preact).astype(jnp.bfloat16)
+            tok.sent[i] = (
+                jnp.dot(hidden, pout.weight[...], preferred_element_type=jnp.float32)
+                .astype(jnp.bfloat16)
+                .reshape(n_plane, cap, width)
+            )
+            sc.hid_t[:, r] = hidden.T
+
+    def turn():
+        step = n_plane * cap
+
+        @pl.loop(0, n_line)
+        def _(i):
+            r = pl.ds(pl.multiple_of(i * step, step), step)
+            sc.tok_t[:, r] = tok.came[i].reshape(step, width).T
+
+    def backward():
+        step = n_plane * cap
+
+        @pl.loop(0, n_line)
+        def _(i):
+            r = pl.ds(pl.multiple_of(i * step, step), step)
+            downward = right_dot(cot.came[i].reshape(step, width), pout.weight[...])
+            sc.slope[r, :] = (downward * silu_slope(sc.preact[r, :])).astype(jnp.bfloat16)
+
+    def back_copy(d, landing):
+        block, q = (d // 2) % n_line, (d // 8) * 2 + d % 2
+        return remote(
+            tok.sent.at[block, q],
+            sc.returned.at[landing],
+            sc.back_send.at[d],
+            sc.back_recv.at[landing],
+            (dp, d),
+        )
+
+    def back_all(what):
         @pl.loop(1, n_expert)
         def _(j):
             d = peer(j)
-            remote(src.at[d], dst.at[me], send.at[d], recv.at[me], (dp, d)).start()
-
-        dst[me] = src[me]
-
-    def all_recv(src, dst, send, recv):
+            if what == "start":
+                back_copy(d, me).start()
+            elif what == "recv":
+                back_copy(d, d).wait_recv()
+            else:
+                back_copy(d, me).wait_send()
+
+    def all_wait(src, dst, send, recv, sent):
         @pl.loop(1, n_expert)
         def _(j):
             d = peer(j)
-            remote(src.at[d], dst.at[d], send.at[d], recv.at[d], (dp, d)).wait_recv()
-
-    def all_sent(src, dst, send, recv):
-        @pl.loop(1, n_expert)
-        def _(j):
-            d = peer(j)
-            remote(src.at[d], dst.at[d], send.at[d], recv.at[d], (dp, d)).wait_send()
+            copy = remote(src.at[d], dst.at[d], send.at[d], recv.at[d], (dp, d))
+            copy.wait_send() if sent else copy.wait_recv()
 
     def ring_copies(p, part):
         def side(block, half):
@@ -194,7 +433,7 @@
             def _(i):
                 r = pl.ds(pl.multiple_of(base + i * step, 16), step)
                 p.partial[r, :] = jnp.dot(
-                    left[r, :], right[...], preferred_element_type=jnp.float32
+                    left[r, :], right(), preferred_element_type=jnp.float32
                 ).astype(jnp.bfloat16)
 
         copies = ring_copies(p, part)
@@ -257,13 +496,15 @@
             for half in range(2):
                 p.own[q, pl.ds(half * part.side, part.side)] = total(half, zh * part.share, i, 0)
 
-    def hop_first(p, part, weight, mean, square):
+    def hop_first(p, part):
         pair_copy(p).wait_recv()
 
         def piece(i):
             at = part.where(i)
+            r = (i // part.per_row) * part.piece[0] + dp * part.share
+            weight = p.weight[pl.ds(pl.multiple_of(r, 16), part.piece[0]), at[1]]
             gradient = p.own[at] + p.pair_in[at].astype(jnp.float32)
-            after = adam_apply(weight[at], mean[at], square[at], gradient)
+            after = adam_apply(weight, p.mean[at], p.square[at], gradient)
             for k in range(3):
                 p.stage[i, k] = after[k]
 
@@ -279,20 +520,21 @@
         p.hop_one[me] = p.stage[me]
 
     def hop_second(p, part):
-        all_recv(p.stage, p.hop_one, p.one_send, p.one_recv)
+        all_wait(p.stage, p.hop_one, p.one_send, p.one_recv, True)
+        all_wait(p.stage, p.hop_one, p.one_send, p.one_recv, False)
 
         @pl.loop(1, n_expert)
         def _(j):
             d = peer(j)
-            p.ordered[d] = p.hop_one[source_of[d]]
+            p.stage[d] = p.hop_one[source_of[d]]
             remote(
-                p.ordered.at[d], p.hop_two.at[me], p.two_send.at[d], p.two_recv.at[me], (dp, d)
+                p.stage.at[d], p.hop_two.at[me], p.two_send.at[d], p.two_recv.at[me], (dp, d)
             ).start()
 
         p.hop_two[me] = p.hop_one[source_of[me]]
 
     def arrive(p, part, results):
-        all_recv(p.ordered, p.hop_two, p.two_send, p.two_recv)
+        all_wait(p.stage, p.hop_two, p.two_send, p.two_recv, False)
 
         @pl.loop(0, n_expert)
         def _(i):
@@ -301,41 +543,68 @@
                 results[k][at] = p.hop_two[i, k]
 
     def mix():
-        all_recv(produced, returned, back_send, back_recv)
-        tok_rows = slot.shape[0]
-        width = produced.shape[2]
-        cap = produced.shape[1]
-        back = returned[...].reshape(n_expert * cap, width)
-        lanes = lax.broadcasted_iota(jnp.int32, (tok_rows, n_expert * cap), 1)
+        back_all("recv")
+        back = sc.returned[...].reshape(slots, width)
+        lanes = lax.broadcasted_iota(jnp.int32, (rows, slots), 1).astype(jnp.float32)
         total = None
         for k in range(2):
-            pick = (slot[:, k : k + 1] == lanes).astype(jnp.float32).astype(jnp.bfloat16)
+            pick = (sc.table[:, k : k + 1] == lanes).astype(jnp.float32).astype(jnp.bfloat16)
             term = gates[:, k : k + 1] * jnp.dot(pick, back, preferred_element_type=jnp.float32)
             total = term if total is None else total + term
         mixed[...] = total.astype(jnp.bfloat16)
 
-    part_in, part_out = parts
-    ring_first(pout, part_out, hid_t, upstream)
-    all_send(produced, returned, back_send, back_recv)
-    ring_first(pin, part_in, tok_t, slope)
+    load(0).wait()
+    z_first(tok)
+    y_send(tok, zl)
+    load(1).wait()
+    z_step(tok, 0)
+    z_first(cot)
+    y_step(tok, 0)
+
+    @pl.loop(1, n_line - 1)
+    def _(step):
+        z_step(tok, step)
+        y_step(tok, step)
+
+    y_send(cot, zl)
+    z_step(cot, 0)
+    y_step(cot, 0)
+    for k in range(2, 8):
+        load(k).wait()
+    forward()
+
+    @pl.loop(1, n_line - 1)
+    def _(step):
+        z_step(cot, step)
+        y_step(cot, step)
+
+    turn()
+    y_all(cot, False)
+    ring_first(pout, part_out, sc.hid_t, lambda: cot.came[...].reshape(slots, width))
+    back_all("start")
+    sc.returned[me] = tok.sent[zl, mine]
+    backward()
+    ring_first(pin, part_in, sc.tok_t, lambda: sc.slope[...])
     ring_second(pout, part_out)
     ring_second(pin, part_in)
     ring_third(pout, part_out)
     ring_third(pin, part_in)
     mix()
-    hop_first(pout, part_out, w_out, m_out, s_out)
-    hop_first(pin, part_in, w_in, m_in, s_in)
+    hop_first(pout, part_out)
+    hop_first(pin, part_in)
     hop_second(pout, part_out)
     hop_second(pin, part_in)
     arrive(pout, part_out, outs[4:7])
     arrive(pin, part_in, outs[1:4])
-    all_sent(produced, returned, back_send, back_recv)
+    z_sent(tok)
+    z_sent(cot)
+    y_all(cot, True)
+    back_all("sent")
     for p, part in ((pout, part_out), (pin, part_in)):
         for k in range(6):
             ring_copies(p, part)(k).wait_send()
         pair_copy(p).wait_send()
-        all_sent(p.stage, p.hop_one, p.one_send, p.one_recv)
-        all_sent(p.ordered, p.hop_two, p.two_send, p.two_recv)
+        all_wait(p.stage, p.hop_two, p.two_send, p.two_recv, True)
 
 
 def body(
@@ -354,94 +623,53 @@
 ):
     n_expert = lax.axis_size("expert")
     n_groups = lax.axis_size("dp")
-    group = lax.axis_index("dp")
     tok_rows, width = tokens.shape
     picks_each = route_ids.shape[1]
     hidden_width = weight_in.shape[2]
     capacity = 2 * tok_rows * picks_each // n_expert
-    slots_all = n_expert * capacity
     rows_in = width // n_groups
     rows_out = hidden_width // n_groups
     experts_all = jnp.arange(n_expert, dtype=jnp.int32)
-    picked = (route_ids[:, :, None] == experts_all[None, None, :]).astype(jnp.int32)
-    counts = jnp.sum(picked, axis=1)
-    before = jnp.cumsum(counts, axis=0) - counts
-    position = jnp.sum(picked * before[:, None, :], axis=2)
-    slot = jnp.sum(picked * old_owner, axis=2) * capacity + position
     holder = (new_owner[:, None] == experts_all[None, :]).astype(jnp.int32)
     source_of = jnp.sum(holder * old_owner[:, None], axis=0)
-    slot_ids = jnp.arange(slots_all, dtype=jnp.int32)
-    place = [
-        (slot[:, k][None, :] == slot_ids[:, None]).astype(jnp.bfloat16) for k in range(picks_each)
-    ]
-
-    def swap(rows):
-        return lax.all_to_all(rows, "expert", split_axis=0, concat_axis=0, tiled=True)
-
-    def exchange(rows):
-        return swap(rows.reshape(n_expert, capacity, width)).reshape(slots_all, width)
-
-    sent = jnp.dot(sum(place), tokens, preferred_element_type=jnp.float32).astype(jnp.bfloat16)
-    arrived = exchange(sent)
-    scaled = [
-        (route_gates[:, k, None] * cotangent.astype(jnp.float32)).astype(jnp.bfloat16)
-        for k in range(picks_each)
-    ]
-    graded = jnp.dot(
-        jnp.concatenate(place, axis=1),
-        jnp.concatenate(scaled, axis=0),
-        preferred_element_type=jnp.float32,
-    ).astype(jnp.bfloat16)
-    upstream = exchange(graded)
-    preact = jnp.dot(arrived, weight_in[0], preferred_element_type=jnp.float32)
-    hidden = jax.nn.silu(preact).astype(jnp.bfloat16)
-    produced = jnp.dot(hidden, weight_out[0], preferred_element_type=jnp.float32).astype(
-        jnp.bfloat16
-    )
-    downward = right_dot(upstream, weight_out[0])
-    slope = (downward * silu_slope(preact)).astype(jnp.bfloat16)
-    in_share = lax.dynamic_slice_in_dim(weight_in[0], group * rows_in, rows_in, 0)
-    out_share = lax.dynamic_slice_in_dim(weight_out[0], group * rows_out, rows_out, 0)
-
     parts = (
         Part(width, hidden_width, (16, hidden_width // 2)),
         Part(hidden_width, width, (rows_out // 2, 128)),
     )
     vmem = pl.BlockSpec(memory_space=pltpu.VMEM)
     smem = pl.BlockSpec(memory_space=pltpu.SMEM)
+    far = pl.BlockSpec(memory_space=pl.ANY)
     shares_in = jax.ShapeDtypeStruct((rows_in, hidden_width), jnp.bfloat16)
     shares_out = jax.ShapeDtypeStruct((rows_out, width), jnp.bfloat16)
+    flow = list(flow_scratch(tok_rows, capacity, width).values())
+    other = other_scratch(tok_rows, capacity, width, hidden_width, n_expert)
     results = pl.pallas_call(
-        functools.partial(finish_kernel, n_expert, parts),
+        functools.partial(whole_kernel, n_expert, parts),
         out_shape=[jax.ShapeDtypeStruct((tok_rows, width), jnp.bfloat16)]
         + [shares_in] * 3
         + [shares_out] * 3,
-        in_specs=[smem] + [vmem] * 13,
+        in_specs=[smem] + [vmem] * 3 + [far] * 8,
         out_specs=[vmem] * 7,
-        scratch_shapes=[
-            pltpu.VMEM((n_expert, capacity, width), jnp.bfloat16),
-            pltpu.SemaphoreType.DMA((n_expert,)),
-            pltpu.SemaphoreType.DMA((n_expert,)),
-        ]
+        scratch_shapes=flow
+        + flow
+        + list(other.values())
         + list(parts[0].scratch(n_expert).values())
         + list(parts[1].scratch(n_expert).values()),
         compiler_params=pltpu.CompilerParams(
-            collective_id=0, has_side_effects=True, vmem_limit_bytes=60 << 20
+            collective_id=0, has_side_effects=True, vmem_limit_bytes=63 << 20
         ),
-        name="finish",
+        name="whole",
     )(
         source_of,
-        slot,
+        old_owner.reshape(1, n_expert),
+        route_ids,
         route_gates,
-        produced.reshape(n_expert, capacity, width),
-        arrived.T,
-        slope,
-        hidden.T,
-        upstream,
-        in_share,
+        tokens,
+        cotangent,
+        weight_in[0],
         mean_in[0],
         square_in[0],
-        out_share,
+        weight_out[0],
         mean_out[0],
         square_out[0],
     )

time: 337 us -> 302 us (0.90)
  Pallas kernels: 198 us -> 286 us
  waiting for transfers between devices: 76.2 us -> 0 us
  matrix products: 20.3 us -> 0 us
  starting transfers between devices: 14.3 us -> 0 us
  local copies, waits for them, and re-layouts: 18.4 us -> 12.3 us
  other arithmetic: 5.06 us -> 1.27 us
    pallas_call x1, Pallas kernels: 198 us -> 286 us  [body(): pl.pallas_call(functools.partial(whole_kernel, n_expert, parts), out_shap...]
    all_to_all x2 -> x0, waiting for transfers between devices: 76.2 us -> none  [swap(): lax.all_to_all(rows, 'expert', split_axis=0, concat_axis=0, tiled=True)]
    dot_general x5 -> x0, matrix products: 20.3 us -> none  [the longest x1 5.54 us: body(): preact = jnp.dot(arrived, weight_in[0], preferred_element_type=jnp.float32)]
    all_to_all x2 -> x0, starting transfers between devices: 14.3 us -> none  [swap(): lax.all_to_all(rows, 'expert', split_axis=0, concat_axis=0, tiled=True)]
    unnamed x30 -> x15, local copies, waits for them, and re-layouts: 8.33 us -> 12.3 us
    reshape x1 -> x0, local copies, waits for them, and re-layouts: 3.93 us -> none  [exchange(): swap(rows.reshape(n_expert, capacity, width)).reshape(slots_all, width)]
  transfers between devices with their start and end apart: 2 -> 0, of which waited for: 2 -> 0; matrix products, arithmetic and copies ran while one was open for 7% -> 0% of each run, Pallas kernels for 0% -> 0%
where the time goes in v3:
time: 302 us; the launch traced here: 300 us
  Pallas kernels  286 us (95%)
  local copies, waits for them, and re-layouts  12.3 us (4%)
    pallas_call x1, Pallas kernels, body(): pl.pallas_call(functools.partial(whole_kernel, n_expert, parts), out_shap...  286 us
    unnamed x15, local copies, waits for them, and re-layouts  12.3 us

profile of v3, /device:TPU:4, one launch (start us, length us, event | category | flops | bytes accessed | tf_op | source)
XLA Modules:
  0.0 300.1 jit_solution(16022397004284747757)
XLA Ops:
  0.6 1.3 select_reduce_fusion.refs_0_
  1.9 1.4 copy.21.refs_2_
  3.3 1.4 copy.22.refs_3_
  4.7 285.8 %whole.1 = (bf16[128,2048]{1,0:T(8,128)(2,1)}, bf16[256,768]{1,0:T(8,128)(2,1)}, bf16[256,768]{1,0:T(8,128)(2,1)}, bf16[256,768]{1,0:T(8,128)(2,1)}, bf16[96,204...) custom-call(s32[32]{0:T(128)} %select_reduce_fusion.refs_0_, s32[1,32]{1,0:T(1,128)} %bitcast.25, ...), custom_call_target="tpu_custom_call" | custom-call | tf_op jit(solution)/shard_map/whole/pallas_call | solution.py:646
  290.6 0.0 copy-start.2
  290.6 0.0 copy-start.1
  290.6 0.0 copy-start
  290.6 2.0 copy.30
  292.6 1.8 copy.31
  294.3 1.8 copy.32
  296.1 1.8 copy.33
  297.9 0.0 copy-done.2
  297.9 0.7 copy.34
  298.6 0.0 copy-done.1
  298.6 0.7 copy.35
  299.4 0.0 copy-done
  299.4 0.7 copy.36
Async XLA Ops:
  290.6 7.3 %copy-start.2 = (bf16[96,2048]{1,0:T(8,128)(2,1)S(1)}, bf16[96,2048]{1,0:T(8,128)(2,1)}, u32[]{:S(2)}) copy-start(bf16[96,2048]{1,0:T(8,128)(2,1)} %get-tuple-element.18) | copy-start | bytes 1179652
  290.6 8.0 %copy-start.1 = (bf16[96,2048]{1,0:T(8,128)(2,1)S(1)}, bf16[96,2048]{1,0:T(8,128)(2,1)}, u32[]{:S(2)}) copy-start(bf16[96,2048]{1,0:T(8,128)(2,1)} %get-tuple-element.19) | copy-start | bytes 1179652
  290.6 8.8 %copy-start = (bf16[96,2048]{1,0:T(8,128)(2,1)S(1)}, bf16[96,2048]{1,0:T(8,128)(2,1)}, u32[]{:S(2)}) copy-start(bf16[96,2048]{1,0:T(8,128)(2,1)} %get-tuple-element.20) | copy-start | bytes 1179652

commit v4 on v3

--- a/solution.py
+++ b/solution.py
@@ -22,16 +22,19 @@
     return logistic * (1.0 + preact * (1.0 - logistic))
 
 
-def adam_apply(weight, mean_old, square_old, gradient):
+def adam_moments(mean_old, square_old, gradient):
     mean_new = beta_one * mean_old.astype(jnp.float32) + (1.0 - beta_one) * gradient
     square_new = beta_two * square_old.astype(jnp.float32) + (1.0 - beta_two) * gradient * gradient
+    return mean_new.astype(jnp.bfloat16), square_new.astype(jnp.bfloat16)
+
+
+def adam_weight(weight, mean_new, square_new):
     stride = (
-        mean_new
+        mean_new.astype(jnp.float32)
         / (1.0 - beta_one**adam_step)
-        / (jnp.sqrt(square_new / (1.0 - beta_two**adam_step)) + adam_eps)
+        / (jnp.sqrt(square_new.astype(jnp.float32) / (1.0 - beta_two**adam_step)) + adam_eps)
     )
-    fresh = (weight.astype(jnp.float32) - learn_rate * stride).astype(jnp.bfloat16)
-    return (fresh, mean_new.astype(jnp.bfloat16), square_new.astype(jnp.bfloat16))
+    return (weight.astype(jnp.float32) - learn_rate * stride).astype(jnp.bfloat16)
 
 
 def outer_dot(left, right):
@@ -74,9 +77,16 @@
             own=pltpu.VMEM((self.share, self.cols), jnp.float32),
             pair_out=pltpu.VMEM((self.share, self.cols), jnp.bfloat16),
             pair_in=pltpu.VMEM((self.share, self.cols), jnp.bfloat16),
-            stage=pltpu.VMEM((n_expert, 3) + self.piece, jnp.bfloat16),
-            hop_one=pltpu.VMEM((n_expert, 3) + self.piece, jnp.bfloat16),
-            hop_two=pltpu.VMEM((n_expert, 3) + self.piece, jnp.bfloat16),
+            stage=pltpu.VMEM((n_expert, 2) + self.piece, jnp.bfloat16),
+            hop_one=pltpu.VMEM((n_expert, 2) + self.piece, jnp.bfloat16),
+            hop_two=pltpu.VMEM((n_expert, 2) + self.piece, jnp.bfloat16),
+            w_one=pltpu.VMEM((n_expert,) + self.piece, jnp.bfloat16),
+            w_stage=pltpu.VMEM((n_expert,) + self.piece, jnp.bfloat16),
+            w_two=pltpu.VMEM((n_expert,) + self.piece, jnp.bfloat16),
+            w_one_send=pltpu.SemaphoreType.DMA((n_expert,)),
+            w_one_recv=pltpu.SemaphoreType.DMA((n_expert,)),
+            w_two_send=pltpu.SemaphoreType.DMA((n_expert,)),
+            w_two_recv=pltpu.SemaphoreType.DMA((n_expert,)),
             weight=pltpu.VMEM((self.rows, self.cols), jnp.bfloat16),
             mean=pltpu.VMEM((self.share, self.cols), jnp.bfloat16),
             square=pltpu.VMEM((self.share, self.cols), jnp.bfloat16),
@@ -119,7 +129,6 @@
         meta=pltpu.VMEM((n_line, 8, rows), jnp.float32),
         meta_send=pltpu.SemaphoreType.DMA((2, n_line)),
         meta_recv=pltpu.SemaphoreType.DMA((n_line,)),
-        table=pltpu.VMEM((rows, 128), jnp.float32),
         preact=pltpu.VMEM((slots, hidden), jnp.float32),
         hid_t=pltpu.VMEM((hidden, slots), jnp.bfloat16),
         tok_t=pltpu.VMEM((width, slots), jnp.bfloat16),
@@ -184,6 +193,14 @@
     def peer(j):
         return (me + j) % n_expert
 
+    def other_half(i):
+        apart = (i // 2) % n_line - zl
+        return (
+            (apart == 3)
+            | (apart == -3)
+            | (((apart == 2) | (apart == -2)) & (i % 2 == me % 2))
+        )
+
     def loads():
         plan = [
             (tokens, tok.raw.at[zl], tok.load),
@@ -209,9 +226,21 @@
     for device in (to_ahead, to_behind, to_pair):
         pl.semaphore_signal(barrier, inc=1, device_id=device, device_id_type=MESH)
 
+    @pl.loop(0, n_expert)
+    def _(i):
+        @pl.when(other_half(i))
+        def _():
+            pl.semaphore_signal(
+                barrier, inc=1, device_id=(x * 2 + 1 - zh, i), device_id_type=MESH
+            )
+
+
     def place_own():
-        lanes = lax.broadcasted_iota(jnp.int32, (rows, n_expert), 1)
-        picked = [(route_ids[:, k : k + 1] == lanes).astype(jnp.float32) for k in range(2)]
+        def column(ref, k):
+            return jnp.broadcast_to(ref[k : k + 1, :].astype(jnp.float32), (rows, rows)).T
+
+        lanes = lax.broadcasted_iota(jnp.int32, (rows, n_expert), 1).astype(jnp.float32)
+        picked = [(column(route_ids, k)[:, 0:1] == lanes).astype(jnp.float32) for k in range(2)]
         earlier = (
             lax.broadcasted_iota(jnp.int32, (rows, rows), 1)
             < lax.broadcasted_iota(jnp.int32, (rows, rows), 0)
@@ -227,13 +256,13 @@
         table = jnp.where(
             lane == 0,
             slot[0],
-            jnp.where(lane == 1, slot[1], jnp.where(lane == 2, gates[:, 0:1], gates[:, 1:2])),
+            jnp.where(lane == 1, slot[1], jnp.where(lane == 2, column(gates, 0), column(gates, 1))),
         )
-        sc.table[...] = table
         sc.meta[zl] = table.T[0:8, :]
 
     place_own()
-    pl.semaphore_wait(barrier, peers + 3)
+    far_half = jnp.where((zl == 0) | (zl == n_line - 1), 12, 4)
+    pl.semaphore_wait(barrier, peers + 3 + far_half)
 
     def z_copies(buf, send, recv, direction, block):
         neighbour = (dp, me + 2 if direction == 0 else me - 2)
@@ -396,6 +425,22 @@
             else:
                 back_copy(d, me).wait_send()
 
+        if what == "start":
+            sc.returned[me] = tok.sent[zl, mine]
+
+    def mix():
+        back_all("recv")
+        back = sc.returned[...].reshape(slots, width)
+        lanes = lax.broadcasted_iota(jnp.int32, (rows, slots), 1).astype(jnp.float32)
+        total = None
+        for k in range(2):
+            slot = jnp.broadcast_to(sc.meta[zl, k : k + 1, :], (rows, rows)).T[:, 0:1]
+            gate = jnp.broadcast_to(sc.meta[zl, 2 + k : 3 + k, :], (rows, rows)).T[:, 0:1]
+            pick = (slot == lanes).astype(jnp.float32).astype(jnp.bfloat16)
+            term = gate * jnp.dot(pick, back, preferred_element_type=jnp.float32)
+            total = term if total is None else total + term
+        mixed[...] = total.astype(jnp.bfloat16)
+
     def all_wait(src, dst, send, recv, sent):
         @pl.loop(1, n_expert)
         def _(j):
@@ -496,16 +541,48 @@
             for half in range(2):
                 p.own[q, pl.ds(half * part.side, part.side)] = total(half, zh * part.share, i, 0)
 
+    def w_copy(p, part, i):
+        to = x * 2 + jnp.where(other_half(i), 1 - zh, zh)
+        at = part.where(i)
+        r = (i // part.per_row) * part.piece[0] + to * part.share
+        source = p.weight.at[pl.ds(pl.multiple_of(r, 16), part.piece[0]), at[1]]
+        return remote(source, p.w_one.at[me], p.w_one_send.at[i], p.w_one_recv.at[me], (to, i))
+
+    def w_first(p, part):
+        @pl.loop(1, n_expert)
+        def _(j):
+            w_copy(p, part, peer(j)).start()
+
+        at = part.where(me)
+        r = (me // part.per_row) * part.piece[0] + dp * part.share
+        p.w_one[me] = p.weight[pl.ds(pl.multiple_of(r, 16), part.piece[0]), at[1]]
+
+    def w_sent(p, part):
+        @pl.loop(1, n_expert)
+        def _(j):
+            w_copy(p, part, peer(j)).wait_send()
+
+    def w_second(p, part):
+        all_wait(p.w_stage, p.w_one, p.w_one_send, p.w_one_recv, False)
+
+        @pl.loop(1, n_expert)
+        def _(j):
+            d = peer(j)
+            p.w_stage[d] = p.w_one[source_of[d]]
+            remote(
+                p.w_stage.at[d], p.w_two.at[me], p.w_two_send.at[d], p.w_two_recv.at[me], (dp, d)
+            ).start()
+
+        p.w_two[me] = p.w_one[source_of[me]]
+
     def hop_first(p, part):
         pair_copy(p).wait_recv()
 
         def piece(i):
             at = part.where(i)
-            r = (i // part.per_row) * part.piece[0] + dp * part.share
-            weight = p.weight[pl.ds(pl.multiple_of(r, 16), part.piece[0]), at[1]]
             gradient = p.own[at] + p.pair_in[at].astype(jnp.float32)
-            after = adam_apply(weight, p.mean[at], p.square[at], gradient)
-            for k in range(3):
+            after = adam_moments(p.mean[at], p.square[at], gradient)
+            for k in range(2):
                 p.stage[i, k] = after[k]
 
         @pl.loop(1, n_expert)
@@ -535,28 +612,20 @@
 
     def arrive(p, part, results):
         all_wait(p.stage, p.hop_two, p.two_send, p.two_recv, False)
+        all_wait(p.w_stage, p.w_two, p.w_two_send, p.w_two_recv, False)
 
         @pl.loop(0, n_expert)
         def _(i):
             at = part.where(i)
-            for k in range(3):
-                results[k][at] = p.hop_two[i, k]
-
-    def mix():
-        back_all("recv")
-        back = sc.returned[...].reshape(slots, width)
-        lanes = lax.broadcasted_iota(jnp.int32, (rows, slots), 1).astype(jnp.float32)
-        total = None
-        for k in range(2):
-            pick = (sc.table[:, k : k + 1] == lanes).astype(jnp.float32).astype(jnp.bfloat16)
-            term = gates[:, k : k + 1] * jnp.dot(pick, back, preferred_element_type=jnp.float32)
-            total = term if total is None else total + term
-        mixed[...] = total.astype(jnp.bfloat16)
+            for k in range(2):
+                results[1 + k][at] = p.hop_two[i, k]
+            results[0][at] = adam_weight(p.w_two[i], p.hop_two[i, 0], p.hop_two[i, 1])
 
     load(0).wait()
     z_first(tok)
     y_send(tok, zl)
     load(1).wait()
+    y_send(cot, zl)
     z_step(tok, 0)
     z_first(cot)
     y_step(tok, 0)
@@ -566,45 +635,62 @@
         z_step(tok, step)
         y_step(tok, step)
 
-    y_send(cot, zl)
     z_step(cot, 0)
     y_step(cot, 0)
     for k in range(2, 8):
         load(k).wait()
     forward()
-
-    @pl.loop(1, n_line - 1)
-    def _(step):
-        z_step(cot, step)
-        y_step(cot, step)
-
+    z_step(cot, 1)
+    w_first(pin, part_in)
+    w_first(pout, part_out)
+    y_step(cot, 1)
     turn()
+    z_step(cot, 2)
+    back_all("start")
+    y_step(cot, 2)
     y_all(cot, False)
     ring_first(pout, part_out, sc.hid_t, lambda: cot.came[...].reshape(slots, width))
-    back_all("start")
-    sc.returned[me] = tok.sent[zl, mine]
     backward()
+    ring_second(pout, part_out)
     ring_first(pin, part_in, sc.tok_t, lambda: sc.slope[...])
-    ring_second(pout, part_out)
+    w_second(pin, part_in)
+    w_second(pout, part_out)
+    ring_third(pout, part_out)
     ring_second(pin, part_in)
-    ring_third(pout, part_out)
+    hop_first(pout, part_out)
     ring_third(pin, part_in)
-    mix()
-    hop_first(pout, part_out)
     hop_first(pin, part_in)
     hop_second(pout, part_out)
     hop_second(pin, part_in)
+    mix()
     arrive(pout, part_out, outs[4:7])
     arrive(pin, part_in, outs[1:4])
-    z_sent(tok)
     z_sent(cot)
     y_all(cot, True)
     back_all("sent")
+    z_sent(tok)
     for p, part in ((pout, part_out), (pin, part_in)):
         for k in range(6):
             ring_copies(p, part)(k).wait_send()
         pair_copy(p).wait_send()
         all_wait(p.stage, p.hop_two, p.two_send, p.two_recv, True)
+        w_sent(p, part)
+        all_wait(p.w_stage, p.w_two, p.w_two_send, p.w_two_recv, True)
+
+
+def store_kernel(*refs):
+    n = (len(refs) - 1) // 3
+    sources, targets, held = refs[:n], refs[n : 2 * n], refs[2 * n : 3 * n]
+    sem = refs[3 * n]
+    fetch = [pltpu.make_async_copy(sources[k], held[k], sem.at[k]) for k in range(n)]
+    put = [pltpu.make_async_copy(held[k], targets[k], sem.at[n + k]) for k in range(n)]
+    for copy in fetch:
+        copy.start()
+    for k in range(n):
+        fetch[k].wait()
+        put[k].start()
+    for copy in put:
+        copy.wait()
 
 
 def body(
@@ -662,8 +748,8 @@
     )(
         source_of,
         old_owner.reshape(1, n_expert),
-        route_ids,
-        route_gates,
+        route_ids.T,
+        route_gates.T,
         tokens,
         cotangent,
         weight_in[0],
@@ -673,6 +759,15 @@
         mean_out[0],
         square_out[0],
     )
+    results = pl.pallas_call(
+        store_kernel,
+        out_shape=[jax.ShapeDtypeStruct(piece.shape, piece.dtype) for piece in results],
+        in_specs=[far] * 7,
+        out_specs=[far] * 7,
+        scratch_shapes=[pltpu.VMEM(piece.shape, piece.dtype) for piece in results]
+        + [pltpu.SemaphoreType.DMA((14,))],
+        name="store",
+    )(*results)
     return (results[0],) + tuple(piece[None] for piece in results[1:])
 
 

time: 302 us -> 262 us (0.87)
  Pallas kernels: 286 us -> 259 us
  local copies, waits for them, and re-layouts: 12.3 us -> 0 us
    pallas_call x1, Pallas kernels: 286 us -> 256 us  [body(): pl.pallas_call(functools.partial(whole_kernel, n_expert, parts), out_shap...]
    unnamed x15 -> x0, local copies, waits for them, and re-layouts: 12.3 us -> none
where the time goes in v4:
time: 262 us; the launch traced here: 261 us
  Pallas kernels  259 us (99%)
    pallas_call x1, Pallas kernels, body(): pl.pallas_call(functools.partial(whole_kernel, n_expert, parts), out_shap...  256 us

profile of v4, /device:TPU:4, one launch (start us, length us, event | category | flops | bytes accessed | tf_op | source)
XLA Modules:
  0.0 261.0 jit_solution(6837719970146896124)
XLA Ops:
  0.6 1.3 select_reduce_fusion.refs_0_
  1.9 256.2 %whole.1 = (bf16[128,2048]{1,0:T(8,128)(2,1)}, bf16[256,768]{1,0:T(8,128)(2,1)}, bf16[256,768]{1,0:T(8,128)(2,1)}, bf16[256,768]{1,0:T(8,128)(2,1)}, bf16[96,204...) custom-call(s32[32]{0:T(128)} %select_reduce_fusion.refs_0_, s32[1,32]{1,0:T(1,128)} %bitcast.23, ...), custom_call_target="tpu_custom_call" | custom-call | tf_op jit(solution)/shard_map/whole/pallas_call | solution.py:732
  258.1 2.7 %store.1 = (bf16[128,2048]{1,0:T(8,128)(2,1)}, bf16[256,768]{1,0:T(8,128)(2,1)}, bf16[256,768]{1,0:T(8,128)(2,1)}, bf16[256,768]{1,0:T(8,128)(2,1)}, bf16[96,204...) custom-call(bf16[128,2048]{1,0:T(8,128)(2,1)} %get-tuple-element.21.refs_0_, ...), custom_call_target="tpu_custom_call" | custom-call | tf_op jit(solution)/shard_map/store/pallas_call | solution.py:762

commit v5 on v4

--- a/solution.py
+++ b/solution.py
@@ -611,15 +611,24 @@
         p.hop_two[me] = p.hop_one[source_of[me]]
 
     def arrive(p, part, results):
-        all_wait(p.stage, p.hop_two, p.two_send, p.two_recv, False)
         all_wait(p.w_stage, p.w_two, p.w_two_send, p.w_two_recv, False)
 
-        @pl.loop(0, n_expert)
-        def _(i):
+        def piece(i):
             at = part.where(i)
             for k in range(2):
                 results[1 + k][at] = p.hop_two[i, k]
             results[0][at] = adam_weight(p.w_two[i], p.hop_two[i, 0], p.hop_two[i, 1])
+
+        piece(me)
+
+        @pl.loop(1, n_expert)
+        def _(j):
+            d = peer(j)
+            copy = remote(
+                p.stage.at[d], p.hop_two.at[d], p.two_send.at[d], p.two_recv.at[d], (dp, d)
+            )
+            copy.wait_recv()
+            piece(d)
 
     load(0).wait()
     z_first(tok)
@@ -644,17 +653,17 @@
     w_first(pin, part_in)
     w_first(pout, part_out)
     y_step(cot, 1)
+    back_all("start")
     turn()
     z_step(cot, 2)
-    back_all("start")
     y_step(cot, 2)
     y_all(cot, False)
     ring_first(pout, part_out, sc.hid_t, lambda: cot.came[...].reshape(slots, width))
     backward()
     ring_second(pout, part_out)
-    ring_first(pin, part_in, sc.tok_t, lambda: sc.slope[...])
     w_second(pin, part_in)
     w_second(pout, part_out)
+    ring_first(pin, part_in, sc.tok_t, lambda: sc.slope[...])
     ring_third(pout, part_out)
     ring_second(pin, part_in)
     hop_first(pout, part_out)

time: 262 us -> 257 us (0.981)
  Pallas kernels: 259 us -> 253 us
    pallas_call x1, Pallas kernels: 256 us -> 250 us  [body(): pl.pallas_call(functools.partial(whole_kernel, n_expert, parts), out_shap...]
where the time goes in v5:
time: 257 us; the launch traced here: 255 us
  Pallas kernels  253 us (98%)
    pallas_call x1, Pallas kernels, body(): pl.pallas_call(functools.partial(whole_kernel, n_expert, parts), out_shap...  250 us

profile of v5, /device:TPU:4, one launch (start us, length us, event | category | flops | bytes accessed | tf_op | source)
XLA Modules:
  0.0 254.7 jit_solution(3724072744235475797)
XLA Ops:
  0.6 1.3 select_reduce_fusion.refs_0_
  1.9 249.9 %whole.1 = (bf16[128,2048]{1,0:T(8,128)(2,1)}, bf16[256,768]{1,0:T(8,128)(2,1)}, bf16[256,768]{1,0:T(8,128)(2,1)}, bf16[256,768]{1,0:T(8,128)(2,1)}, bf16[96,204...) custom-call(s32[32]{0:T(128)} %select_reduce_fusion.refs_0_, s32[1,32]{1,0:T(1,128)} %bitcast.23, ...), custom_call_target="tpu_custom_call" | custom-call | tf_op jit(solution)/shard_map/whole/pallas_call | solution.py:741
  251.8 2.7 %store.1 = (bf16[128,2048]{1,0:T(8,128)(2,1)}, bf16[256,768]{1,0:T(8,128)(2,1)}, bf16[256,768]{1,0:T(8,128)(2,1)}, bf16[256,768]{1,0:T(8,128)(2,1)}, bf16[96,204...) custom-call(bf16[128,2048]{1,0:T(8,128)(2,1)} %get-tuple-element.21.refs_0_, ...), custom_call_target="tpu_custom_call" | custom-call | tf_op jit(solution)/shard_map/store/pallas_call | solution.py:771
